TPU v7x, 256 devices: a whole 4x4x8 slice. The times are simulated.
256 devices in a mesh: bin: 16 (over y, x_hi, core), coil: 16 (over z, x_lo).
Axes of the slice: x: 4 (x_hi: 2, x_lo: 2; x = x_hi * 2 + x_lo), y: 4, z: 8, core: 2. Of those that a mesh axis runs over, the one named last changes fastest.
Arguments:
- cine_image: bfloat16 [16, 256, 8, 256], P('bin', 'coil'), may hold values from -6 to 6
- warp_blocks: bfloat16 [16, 4096, 2, 4096], P('bin', 'coil'), may hold values from -0.5 to 0.5
- warp_index: int32 [16, 4096, 2], P('bin', 'coil'), may hold values from 0 to 4095, as said below
- sample_mask: int32 [16, 256, 128], P('bin'), may hold values 0 or 1
- kspace_data: bfloat16 [16, 32, 256, 8, 256], P('bin', 'coil'), may hold values from -6 to 6
- sensitivity: bfloat16 [32, 256, 8, 256], P(None, 'coil'), may hold values from -1.5 to 1.5
Outputs:
- gradient: float32 [16, 256, 8, 256], P('bin', 'coil')
Inputs may be any that keep to these rules, and one draw needn't show every extreme that they name: `warp_index`: slot 0 of every block names the block itself; every other slot of the block at row y names a block whose row lies among the 16 rows from 16 * (y // 16) on.
All inputs are finite; a program needn't handle non-finite values. No bound on the sum of `sample_mask` on one device may be relied on, other than what follows from the above.
Results may differ from a plain program's by a relative error of at most 0.017.
Values may be sent and summed in bfloat16 or wider, within the bound.
No kernel may reach another device: no remote copies, remote signals or barrier semaphores. Data moves between devices by JAX's collectives and lax.ppermute only.
A program may use at most 128 MiB of HBM per device.

v0:
```python
import jax
import jax.numpy as jnp
from jax import lax
from jax.sharding import PartitionSpec as P

NY = 256
NX = 128
BLOCK = 64


def shifted(block, axis, distance):
    devices = range(lax.axis_size(axis))
    route = [((i - distance) % len(devices), i) for i in devices]
    return lax.ppermute(block, axis, route)


def cosine_sine(length):
    positions = jnp.arange(length, dtype=jnp.int32)
    phases = positions[:, None] * positions[None, :] % length
    angles = phases.astype(jnp.float32) * (2.0 * jnp.pi / length)
    factor = 1.0 / jnp.sqrt(jnp.asarray(length, jnp.float32))
    return (jnp.cos(angles) * factor, jnp.sin(angles) * factor)


def make_row_matrix(length):
    cosine_table, sine_table = cosine_sine(length)
    upper_half = jnp.concatenate([cosine_table, -sine_table], axis=1)
    lower_half = jnp.concatenate([sine_table, cosine_table], axis=1)
    return jnp.concatenate([upper_half, lower_half], axis=0).astype(jnp.bfloat16)


def make_column_tables(length):
    cosine_table, sine_table = cosine_sine(length)
    return jnp.stack([cosine_table, sine_table]).astype(jnp.bfloat16)


def row_apply(values, row_matrix, inverse):
    flattened = values.reshape(-1, values.shape[-1])
    table_used = row_matrix.T if inverse else row_matrix
    return jnp.dot(flattened, table_used, preferred_element_type=jnp.float32).reshape(values.shape)


def column_transform(values, tables, inverse):
    products = jnp.einsum("tky,cyzx->tckzx", tables, values, preferred_element_type=jnp.float32)
    direct, turned = (products[0], products[1])
    half_width = direct.shape[-1] // 2
    if inverse:
        swapped = jnp.concatenate([-turned[..., half_width:], turned[..., :half_width]], axis=-1)
    else:
        swapped = jnp.concatenate([turned[..., half_width:], -turned[..., :half_width]], axis=-1)
    return direct + swapped


def coil_images(sensitivity, moved_image):
    half_width = moved_image.shape[-1] // 2
    sens_re = sensitivity[..., :half_width].astype(jnp.float32)
    sens_im = sensitivity[..., half_width:].astype(jnp.float32)
    image_re = moved_image[..., :half_width].astype(jnp.float32)
    image_im = moved_image[..., half_width:].astype(jnp.float32)
    real_part = sens_re * image_re - sens_im * image_im
    imag_part = sens_re * image_im + sens_im * image_re
    return jnp.concatenate([real_part, imag_part], axis=-1).astype(jnp.bfloat16)


def conj_sum(sensitivity, back_rows):
    half_width = back_rows.shape[-1] // 2
    sens_re = sensitivity[..., :half_width].astype(jnp.float32)
    sens_im = sensitivity[..., half_width:].astype(jnp.float32)
    back_re = back_rows[..., :half_width]
    back_im = back_rows[..., half_width:]
    real_part = jnp.sum(sens_re * back_re + sens_im * back_im, axis=0)
    imag_part = jnp.sum(sens_re * back_im - sens_im * back_re, axis=0)
    return jnp.concatenate([real_part, imag_part], axis=-1)


def column_part(row_spectra, measured, mask_now, column_tables):
    spectra = column_transform(row_spectra, column_tables, False)
    weight_mask = jnp.concatenate([mask_now, mask_now], axis=1).astype(jnp.float32)[:, None, :]
    residual = (weight_mask * (spectra - measured.astype(jnp.float32))).astype(jnp.bfloat16)
    return column_transform(residual, column_tables, True).astype(jnp.bfloat16)


def split_blocks(values):
    row_count, depth_count, full_width = values.shape
    grouped = values.reshape(row_count, depth_count, 2, full_width // (2 * BLOCK), BLOCK)
    return grouped.transpose(0, 1, 3, 2, 4).reshape(-1, 2, BLOCK)


def join_blocks(pieces, row_count, depth_count, full_width):
    grouped = pieces.reshape(row_count, depth_count, full_width // (2 * BLOCK), 2, BLOCK)
    return grouped.transpose(0, 1, 3, 2, 4).reshape(row_count, depth_count, full_width)


def warp_forward(source, weights, block_index):
    pieces = split_blocks(source)
    chosen = jnp.take(pieces, block_index, axis=0)
    matrices = weights.reshape(weights.shape[0], weights.shape[1], BLOCK, BLOCK)
    return jnp.einsum("ikpq,ikcq->icp", matrices, chosen, preferred_element_type=jnp.float32)


def warp_adjoint(values, weights, block_index):
    block_count, slots = block_index.shape
    matrices = weights.reshape(block_count, slots, BLOCK, BLOCK)
    contributions = jnp.einsum(
        "ikpq,icp->ikcq", matrices, values, preferred_element_type=jnp.float32
    )
    targets = jnp.arange(block_count, dtype=jnp.int32)
    selector = (block_index.reshape(1, -1) == targets[:, None]).astype(jnp.float32)
    summed = jnp.dot(
        selector,
        contributions.reshape(block_count * slots, 2 * BLOCK),
        precision=lax.Precision.HIGHEST,
    )
    return summed.reshape(block_count, 2, BLOCK)


def on_device(cine_image, warp_blocks, warp_index, sample_mask, kspace_data, sensitivity):
    current = cine_image[0]
    row_count, depth_count, full_width = current.shape
    row_matrix = make_row_matrix(NX)
    column_tables = make_column_tables(NY)
    earlier = shifted(cine_image, "bin", 1)[0]
    block_count = warp_index.shape[1]
    local_index = warp_index[0] - lax.axis_index("coil") * block_count
    weights = warp_blocks[0]
    warped = join_blocks(
        warp_forward(earlier, weights, local_index), row_count, depth_count, full_width
    )
    moved_image = (current.astype(jnp.float32) + warped).astype(jnp.bfloat16)
    measured = kspace_data[0]
    mask_now = sample_mask[0]
    coil_sens = lax.all_to_all(sensitivity, "coil", split_axis=0, concat_axis=1, tiled=True)
    sens_rows = coil_sens
    images = coil_images(sens_rows, lax.all_gather(moved_image, "coil", axis=0, tiled=True))
    own_coils = row_apply(images, row_matrix, False).astype(jnp.bfloat16)
    back_columns = column_part(own_coils, measured, mask_now, column_tables)
    sens_rows = coil_sens
    data_grad = lax.psum_scatter(
        conj_sum(sens_rows, row_apply(back_columns, row_matrix, True)).astype(jnp.bfloat16),
        "coil",
        scatter_dimension=0,
        tiled=True,
    ).astype(jnp.float32)
    pieces = split_blocks(data_grad.astype(jnp.bfloat16))
    pulled = join_blocks(
        warp_adjoint(pieces, weights, local_index), row_count, depth_count, full_width
    ).astype(jnp.bfloat16)
    from_next = shifted(pulled, "bin", -1)
    return (data_grad + from_next.astype(jnp.float32))[None]


def solution(mesh):
    return jax.shard_map(
        on_device,
        mesh=mesh,
        in_specs=(
            P("bin", "coil", None, None),
            P("bin", "coil", None, None),
            P("bin", "coil", None),
            P("bin", None, None),
            P("bin", "coil", None, None, None),
            P(None, "coil", None, None),
        ),
        out_specs=P("bin", "coil", None, None),
        check_vma=False,
    )
```

profile of v0, /device:TPU:1, one launch (start us, length us, event | category | flops | bytes accessed | tf_op | source)
XLA Modules:
  0.0 242.1 jit_solution(16444079710828115468)
XLA Ops:
  6.5 10.2 %all-to-all-start = ((bf16[32,16,8,256]{3,2,1,0:T(8,128)(2,1)}), bf16[32,16,8,256]{3,2,1,0:T(8,128)(2,1)S(1)}, u32[]{:S(2)}, u32[]{:S(2)}) async-start(bf16[32,16,8,256]{3,2,1,0:T(8,128)(2,1)} %param.11), calls=%async_computation | async-start | bytes 4194304 | tf_op jit(solution)/shard_map/all_to_all | solution.py:132
  16.8 3.4 %collective-permute-start = (bf16[1,16,8,256]{3,2,1,0:T(8,128)(2,1)S(1)}, bf16[1,16,8,256]{3,2,1,0:T(8,128)(2,1)S(1)}, u32[]{:S(2)}, u32[]{:S(2)}) collective-permute-start(bf16[1,16,8,256]{3,2,1,0:T(8,128)(2,1)S(1)} %copy-done.9), channel_id=1, source_target_pairs={{240,0},{0,16},{16,32},{32,48},{48,64},{64,80},{80,96},{96,112},{1... | collective-permute-start | bytes 196616 | tf_op jit(solution)/shard_map/ppermute | solution.py:14
  20.5 11.1 %copy.66 = bf16[1,256,2,4096]{1,3,2,0:T(8,128)(2,1)} copy(bf16[1,256,2,4096]{3,2,1,0:T(2,128)(2,1)} %param.7) | data formatting | bytes 8388608 | tf_op args[1]
  31.5 13.0 %copy.67 = bf16[256,2,64,64]{3,2,1,0:T(8,128)(2,1)} copy(bf16[256,2,64,64]{0,3,2,1:T(8,128)(2,1)} %bitcast.123) | data formatting | bytes 8388608 | tf_op jit(solution)/shard_map/reshape;squeeze | solution.py:97
  45.1 2.1 gather_fusion
  47.2 6.9 %fusion.36 = f32[256,2,64,1]{2,1,3,0:T(2,128)S(1)} fusion(bf16[256,2,64,64]{3,2,1,0:T(8,128)(2,1)} %copy.67, bf16[256,2,2,64]{3,2,1,0:T(2,128)(2,1)S(1)} %bitcast.129, pred[256,2]{1,0:T(8,128)(4,1)S(1)} %copy.62), kind=kOutput, calls=%fused_computation.56 | convolution fusion | flops 8454144 | bytes 4456960 | tf_op jit(solution)/shard_map/ikpq,ikcq->icp/dot_general | solution.py:98
  54.5 0.6 fusion.42
  55.5 4.3 %copy.73 = bf16[1,2,256,8,256]{2,4,3,1,0:T(8,128)(2,1)} copy(bf16[1,2,256,8,256]{4,3,2,1,0:T(8,128)(2,1)} %param.10) | data formatting | bytes 4194304 | tf_op args[4]
  59.9 0.9 fusion.50
  60.8 0.9 negate_convert_fusion
  61.7 1.7 multiply_convert_fusion
  63.4 51.0 %all-gather.2.cloned.1.call-done = bf16[256,8,256]{2,1,0:T(8,128)(2,1)} async-done(((bf16[16,8,256]{2,1,0:T(8,128)(2,1)}), bf16[256,8,256]{2,1,0:T(8,128)(2,1)}) %all-gather.2.cloned.1.call-update) | async-done | bytes 1048592 | tf_op jit(solution)/shard_map/all_gather | solution.py:134
  114.4 1.3 slice_convert_fusion.1
  116.0 1.2 copy.70
  117.1 1.4 copy-done.1
  118.5 2.1 copy.60
  120.7 2.0 fusion.7
  122.7 6.6 %convolution_bitcast_fusion.1 = f32[2,2,256,8,256]{2,4,0,3,1:T(8,128)} fusion(bf16[2,256,8,128]{3,1,2,0:T(8,128)(2,1)} %get-tuple-element.14, bf16[2,256,8,128]{3,1,2,0:T(8,128)(2,1)} %get-tuple-element.13, bf16[1,256,256]{2,1,0:T(8,128)(2,1)S(1)} %get-tuple-element.17, bf16[1,256,256]{2,1,0:T(8,128)(2,1)} %get-tuple-element.18, ...), kind=kOutput, calls=%fused_computation.20 | convolution fusion | flops 1616904192 | bytes 10846208 | tf_op jit(solution)/shard_map/tky,cyzx->tckzx/dot_general | solution.py:44
  129.3 2.7 %slice_bitcast_fusion.2 = f32[2,256,8,256]{1,3,2,0:T(8,128)S(1)} fusion(f32[2,2,256,8,256]{2,4,0,3,1:T(8,128)} %convolution_bitcast_fusion.1), kind=kLoop, calls=%fused_computation.5 | loop fusion | bytes 8388608 | tf_op jit(solution)/shard_map/squeeze | solution.py:45
  132.1 0.4 fusion.58
  132.8 1.7 slice-done.1
  134.5 0.6 copy-done
  135.1 1.4 convolution_bitcast_fusion
  137.6 0.9 fusion.16
  138.5 0.8 fusion.11
  139.3 1.2 pad_maximum_fusion
  140.8 71.2 %reduce-scatter.2.cloned.1.call-done = bf16[16,8,256]{2,0,1:T(8,128)(2,1)} async-done(((bf16[256,8,256]{2,0,1:T(8,128)(2,1)}), bf16[16,8,256]{2,0,1:T(8,128)(2,1)}) %reduce-scatter.2.cloned.1.call-update) | async-done | bytes 65552 | tf_op jit(solution)/shard_map/reduce_scatter | solution.py:138
  212.0 1.0 reshape.200
  213.0 4.6 %convolution_bitcast_fusion.2 = f32[256,2,2,64]{3,2,1,0:T(2,128)S(1)} fusion(bf16[256,2,64,1]{2,1,3,0:T(2,128)(2,1)S(1)} %bitcast.126, bf16[256,2,64,64]{3,2,1,0:T(8,128)(2,1)} %copy.67), kind=kOutput, calls=%fused_computation.41 | convolution fusion | flops 8388608 | bytes 4521984 | tf_op jit(solution)/shard_map/ikpq,icp->ikcq/dot_general | solution.py:104
  218.7 11.6 %collective-permute-start.1 = (bf16[16,8,256]{2,0,1:T(8,128)(2,1)S(1)}, bf16[16,8,256]{2,0,1:T(8,128)(2,1)S(1)}, u32[]{:S(2)}, u32[]{:S(2)}) collective-permute-start(bf16[16,8,256]{2,0,1:T(8,128)(2,1)S(1)} %reshape.222), channel_id=1, source_target_pairs={{16,0},{32,16},{48,32},{64,48},{80,64},{96,80},{112,96},{128,112},... | collective-permute-start | bytes 196616 | tf_op jit(solution)/shard_map/ppermute | solution.py:14
  230.3 4.2 %collective-permute-done.1 = bf16[16,8,256]{2,0,1:T(8,128)(2,1)S(1)} collective-permute-done((bf16[16,8,256]{2,0,1:T(8,128)(2,1)S(1)}, bf16[16,8,256]{2,0,1:T(8,128)(2,1)S(1)}, u32[]{:S(2)}, u32[]{:S(2)}) %collective-permute-start.1) | collective-permute-done | bytes 65568 | tf_op jit(solution)/shard_map/ppermute | solution.py:14
  234.5 0.7 copy.82
  (56 shorter events, 4.8 us)
Async XLA Ops:
  6.5 10.2 %copy-start.9 = (bf16[1,16,8,256]{3,2,1,0:T(8,128)(2,1)S(1)}, bf16[1,16,8,256]{3,2,1,0:T(8,128)(2,1)}, u32[]{:S(2)}) copy-start(bf16[1,16,8,256]{3,2,1,0:T(8,128)(2,1)} %param.6) | copy-start | bytes 196612
  6.5 13.6 %copy-start.10 = (s32[1,256,2]{1,2,0:T(2,128)S(1)}, s32[1,256,2]{1,2,0:T(2,128)}, u32[]{:S(2)}) copy-start(s32[1,256,2]{1,2,0:T(2,128)} %param.8) | copy-start | bytes 6148
  6.5 110.6 %all-to-all-start = ((bf16[32,16,8,256]{3,2,1,0:T(8,128)(2,1)}), bf16[32,16,8,256]{3,2,1,0:T(8,128)(2,1)S(1)}, u32[]{:S(2)}, u32[]{:S(2)}) async-start(bf16[32,16,8,256]{3,2,1,0:T(8,128)(2,1)} %param.11), calls=%async_computation | async-start | bytes 4194304 | tf_op jit(solution)/shard_map/all_to_all | solution.py:132
  16.7 97.7 %all-gather.2.cloned.1.call-start = ((), (), s32[]{:S(2)}) async-start(), calls=%async_computation.2 | async-start | bytes 1114112 | tf_op jit(solution)/shard_map/all_gather | solution.py:134
  16.8 27.9 %collective-permute-start = (bf16[1,16,8,256]{3,2,1,0:T(8,128)(2,1)S(1)}, bf16[1,16,8,256]{3,2,1,0:T(8,128)(2,1)S(1)}, u32[]{:S(2)}, u32[]{:S(2)}) collective-permute-start(bf16[1,16,8,256]{3,2,1,0:T(8,128)(2,1)S(1)} %copy-done.9), channel_id=1, source_target_pairs={{240,0},{0,16},{16,32},{32,48},{48,64},{64,80},{80,96},{96,112},{1... | collective-permute-start | bytes 196616 | tf_op jit(solution)/shard_map/ppermute | solution.py:14
  55.2 4.5 %copy-start.8 = (s32[1,256,128]{2,1,0:T(8,128)S(1)}, s32[1,256,128]{2,1,0:T(8,128)}, u32[]{:S(2)}) copy-start(s32[1,256,128]{2,1,0:T(8,128)} %param.9) | copy-start | bytes 393220
  55.2 156.7 %reduce-scatter.2.cloned.1.call-start = ((), (), s32[]{:S(2)}) async-start(), calls=%async_computation.3 | async-start | bytes 1114112 | tf_op jit(solution)/shard_map/reduce_scatter | solution.py:138
  117.1 1.4 copy-start.1
  118.5 2.1 copy-start.2
  129.3 3.5 %slice-start = ((s8[8388608]{0:T(1024)(128)(4,1)}), s8[4194304]{0:T(1024)(128)(4,1)S(1)}, s32[]{:S(2)}) async-start(s8[8388608]{0:T(1024)(128)(4,1)} %bitcast.119), calls=%async_computation.4 | async-start | bytes 8388608
  132.1 2.4 slice-start.1
  132.1 2.9 %copy-start = (bf16[1,2,256,8,256]{2,4,3,1,0:T(8,128)(2,1)S(1)}, bf16[1,2,256,8,256]{2,4,3,1,0:T(8,128)(2,1)}, u32[]{:S(2)}) copy-start(bf16[1,2,256,8,256]{2,4,3,1,0:T(8,128)(2,1)} %copy.73) | copy-start | bytes 6291460
  132.1 2.9 %copy-start.3 = (bf16[1,256,256]{2,1,0:T(8,128)(2,1)S(1)}, bf16[1,256,256]{2,1,0:T(8,128)(2,1)}, u32[]{:S(2)}) copy-start(bf16[1,256,256]{2,1,0:T(8,128)(2,1)} %get-tuple-element.18) | copy-start | bytes 393220
  136.8 0.8 copy-start.4
  136.8 0.8 copy-start.5
  136.9 0.8 copy-start.6
  217.6 16.9 %copy-start.7 = (bf16[16,8,256]{2,0,1:T(8,128)(2,1)S(1)}, bf16[16,8,256]{2,0,1:T(8,128)(2,1)}, u32[]{:S(2)}) copy-start(bf16[16,8,256]{2,0,1:T(8,128)(2,1)} %reduce-scatter.2.cloned.1.call-done) | copy-start | bytes 196612
  218.7 15.7 %collective-permute-start.1 = (bf16[16,8,256]{2,0,1:T(8,128)(2,1)S(1)}, bf16[16,8,256]{2,0,1:T(8,128)(2,1)S(1)}, u32[]{:S(2)}, u32[]{:S(2)}) collective-permute-start(bf16[16,8,256]{2,0,1:T(8,128)(2,1)S(1)} %reshape.222), channel_id=1, source_target_pairs={{16,0},{32,16},{48,32},{64,48},{80,64},{96,80},{112,96},{128,112},... | collective-permute-start | bytes 196616 | tf_op jit(solution)/shard_map/ppermute | solution.py:14
Sparse Core Ops, SparseCore 0:
  55.3 59.0 all-gather.1
  140.6 71.3 reduce-scatter.1
where the time goes:
time: 243 us; the launch traced here: 242 us
  waiting for transfers between devices  126 us (52%)
  local copies, waits for them, and re-layouts  45.4 us (19%)
  starting transfers between devices  25.4 us (10%)
  matrix products  20.8 us (9%)
  between operations  13.7 us (6%)
  other arithmetic  10.4 us (4%)
    reduce_scatter x1, waiting for transfers between devices, on_device(): lax.psum_scatter(conj_sum(sens_rows, row_apply(back_columns, row_matrix,...  71.2 us
    all_gather x1, waiting for transfers between devices, on_device(): lax.all_gather(moved_image, 'coil', axis=0, tiled=True)  51 us
    unnamed x28, local copies, waits for them, and re-layouts  19.6 us
    ppermute x2, starting transfers between devices, shifted(): return lax.ppermute(block, axis, route)  14.9 us
    another operation x1, local copies, waits for them, and re-layouts, warp_forward(): matrices = weights.reshape(weights.shape[0], weights.shape[1], BLOCK, BLOCK)  13 us
    all_to_all x1, starting transfers between devices, on_device(): lax.all_to_all(sensitivity, 'coil', split_axis=0, concat_axis=1, tiled=True)  10.2 us
    dot_general x2, matrix products, column_transform(): jnp.einsum('tky,cyzx->tckzx', tables, values, preferred_element_type=jnp....  7.98 us
    dot_general x1, matrix products, warp_forward(): jnp.einsum('ikpq,ikcq->icp', matrices, chosen, preferred_element_type=jnp...  6.95 us
  transfers between devices with their start and end apart: 5, of which 3 were waited for; matrix products, arithmetic and copies ran while one was open for 19% of the time, Pallas kernels for 0%

commit v1 on v0

v1 whole, which is shorter than its diff:
```python
import functools

import jax
import jax.numpy as jnp
import numpy as np
from jax import lax
from jax.experimental import pallas as pl
from jax.experimental.pallas import tpu as pltpu
from jax.sharding import Mesh
from jax.sharding import PartitionSpec as P

NY = 256
NX = 128
Z = 8
COILS = 32
SHARE = 4
STEP = 32
PAIR = 2

F32 = jnp.float32
BF16 = jnp.bfloat16


def cosine_sine(length):
    positions = np.arange(length)
    phases = positions[:, None] * positions[None, :] % length
    angles = phases * (2.0 * np.pi / length)
    return np.cos(angles) / np.sqrt(length), np.sin(angles) / np.sqrt(length)


def row_matrix():
    cosine, sine = cosine_sine(NX)
    return np.block([[cosine, -sine], [sine, cosine]]).astype(BF16)


def column_table():
    return np.concatenate(cosine_sine(NY), axis=1).astype(BF16)


def iota(shape, axis):
    return lax.broadcasted_iota(jnp.int32, shape, axis)


def matmul(a, b):
    return jnp.dot(a, b, preferred_element_type=F32)


def high_low(values):
    high = values.astype(BF16)
    return high, (values - high.astype(F32)).astype(BF16)


def sublane_roles(rows):
    r = iota((rows, 128), 0)
    return r, (r >> 2) & 1, (r >> 1) & 1, r & 1


def shift_lanes(values, distance):
    return jnp.where(
        distance == 1,
        pltpu.roll(values, 1, 1),
        jnp.where(distance == -1, pltpu.roll(values, 127, 1), values),
    )


def depth_major():
    to, frm = iota((128, 128), 0), iota((128, 128), 1)
    return ((to & 15) * Z + (to >> 4) == frm).astype(F32).astype(BF16)


def warp_kernel(share, col_ref, w_ref, prior_ref, cur_ref, out_ref, acc_ref):
    step = pl.program_id(0)
    rows = 8 * STEP
    index = col_ref[...]
    r, slot, odd, imag = sublane_roles(rows)
    lane = iota((rows, 128), 1)
    half = lane >> 6
    chosen = (lane == (index >> 1)).astype(F32).astype(BF16)
    both = matmul(chosen, prior_ref[...])
    v = jnp.where(imag == 1, both[:, 128:], both[:, :128])
    v = jnp.where((index & 1) == odd, v, pltpu.roll(v, 64, 1))
    v = jnp.where(half == odd, v, 0.0)
    f = lax.dot_general(
        v.reshape(STEP, 8, 128).astype(BF16),
        w_ref[...],
        (((2,), (2,)), ((0,), (0,))),
        preferred_element_type=F32,
    ).reshape(rows, 64)
    f = jnp.concatenate([f, f], axis=1)
    f = jnp.where((lane & 1) == slot, f, 0.0)
    f = shift_lanes(f, odd - slot)
    f = jnp.where(half == ((r >> 3) & 1), f, 0.0)
    f = jnp.concatenate([jnp.where(imag == 0, f, 0.0), jnp.where(imag == 1, f, 0.0)], axis=1)
    gather = (iota((16, rows), 1) >> 4 == iota((16, rows), 0)).astype(F32).astype(BF16)
    high, low = high_low(f)
    acc_ref[pl.ds(pl.multiple_of(step * 16, 16), 16), :] = matmul(gather, high) + matmul(gather, low)

    @pl.when(step == pl.num_programs(0) - 1)
    def _():
        moved = (cur_ref[...].astype(F32) + acc_ref[...]).astype(BF16)
        turned = matmul(depth_major(), moved).astype(BF16).reshape(share, 128 // share, 256)
        for g in range(16 // share):
            out_ref[g * share : (g + 1) * share] = turned


def adjoint_kernel(share, col_ref, row_ref, w_ref, parts_ref, grad_ref, pulled_ref, image_ref, acc_ref):
    step = pl.program_id(0)
    rows = 8 * STEP

    @pl.when(step == 0)
    def _():
        total = parts_ref[0:share].astype(F32)
        for g in range(1, 16 // share):
            total = total + parts_ref[g * share : (g + 1) * share].astype(F32)
        total = total.reshape(128, 256)
        frm, to = iota((128, 128), 1), iota((128, 128), 0)
        turn = ((frm & 15) * Z + (frm >> 4) == to).astype(F32).astype(BF16)
        high, low = high_low(total)
        lowest = (total - high.astype(F32) - low.astype(F32)).astype(BF16)
        grad = matmul(turn, high) + matmul(turn, low) + matmul(turn, lowest)
        grad_ref[...] = grad
        image_ref[...] = grad.astype(BF16)
        acc_ref[...] = jnp.zeros_like(acc_ref)

    index = col_ref[...]
    r, slot, odd, imag = sublane_roles(rows)
    lane = iota((rows, 128), 1)
    half = lane >> 6
    chosen = (lane == step * (STEP // 2) + (r >> 4)).astype(F32).astype(BF16)
    both = matmul(chosen, image_ref[...])
    v = jnp.where(imag == 1, both[:, 128:], both[:, :128])
    v = jnp.where(half == ((r >> 3) & 1), v, pltpu.roll(v, 64, 1))
    v = jnp.where((lane & 1) == odd, v, 0.0)
    v = shift_lanes(v, slot - odd)
    f = lax.dot_general(
        v[:, :64].reshape(STEP, 8, 64).astype(BF16),
        w_ref[...],
        (((2,), (1,)), ((0,), (0,))),
        preferred_element_type=F32,
    ).reshape(rows, 128)
    f = jnp.where(half == odd, f, 0.0)
    f = f + pltpu.roll(f, 64, 1)
    f = jnp.where(half == (index & 1), f, 0.0)
    f = jnp.concatenate([jnp.where(imag == 0, f, 0.0), jnp.where(imag == 1, f, 0.0)], axis=1)
    scatter = (iota((128, rows), 0) == (row_ref[...] >> 1)).astype(F32).astype(BF16)
    high, low = high_low(f)
    acc_ref[...] += matmul(scatter, high) + matmul(scatter, low)

    @pl.when(step == pl.num_programs(0) - 1)
    def _():
        pulled_ref[...] = acc_ref[...].astype(BF16)


def data_kernel(moved_ref, sens_ref, data_ref, mask_ref, row_ref, back_ref, table_ref, out_ref, acc_ref):
    chunk = pl.program_id(1)
    moved = moved_ref[...].reshape(NY, 256).astype(F32)
    image_re, image_im = moved[:, :NX], moved[:, NX:]
    mask = mask_ref[...].astype(F32)
    table = table_ref[...]
    sens_re, sens_im, images = [], [], []
    for c in range(PAIR):
        sens = sens_ref[:, c].reshape(NY, 256).astype(F32)
        sens_re.append(sens[:, :NX])
        sens_im.append(sens[:, NX:])
        images.append(sens_re[c] * image_re - sens_im[c] * image_im)
        images.append(sens_re[c] * image_im + sens_im[c] * image_re)
    images = [jnp.concatenate(images[2 * c : 2 * c + 2], axis=1).astype(BF16) for c in range(PAIR)]
    spectra = matmul(jnp.concatenate(images, axis=0), row_ref[...])
    tops, bottoms = [], []
    for c in range(PAIR):
        s = spectra[c * NY : (c + 1) * NY]
        tops.append(s)
        bottoms += [s[:, NX:], -s[:, :NX]]
    stacked = jnp.concatenate([jnp.concatenate(tops, axis=1), jnp.concatenate(bottoms, axis=1)], axis=0).astype(BF16)
    spectra = matmul(table, stacked)
    tops, bottoms = [], []
    for c in range(PAIR):
        measured = data_ref[c].reshape(NY, 256).astype(F32)
        s = spectra[:, c * 256 : (c + 1) * 256] - measured
        res_re, res_im = mask * s[:, :NX], mask * s[:, NX:]
        tops += [res_re, res_im]
        bottoms += [-res_im, res_re]
    stacked = jnp.concatenate([jnp.concatenate(tops, axis=1), jnp.concatenate(bottoms, axis=1)], axis=0).astype(BF16)
    columns = matmul(table, stacked).astype(BF16)
    rows = matmul(jnp.concatenate([columns[:, c * 256 : (c + 1) * 256] for c in range(PAIR)], axis=0), back_ref[...])
    real = imag = 0.0
    for c in range(PAIR):
        b = rows[c * NY : (c + 1) * NY]
        back_re, back_im = b[:, :NX], b[:, NX:]
        real += sens_re[c] * back_re + sens_im[c] * back_im
        imag += sens_re[c] * back_im - sens_im[c] * back_re
    both = jnp.concatenate([real, imag], axis=1)
    total = jnp.where(chunk == 0, both, acc_ref[...] + both)
    acc_ref[...] = total
    out_ref[...] = total.astype(BF16).reshape(out_ref.shape)


def full(shape):
    return pl.BlockSpec(shape, lambda *_: (0,) * len(shape))


def warp_forward(share, columns, weights, prior, current):
    return pl.pallas_call(
        functools.partial(warp_kernel, share),
        grid=(256 // STEP,),
        in_specs=[
            pl.BlockSpec((8 * STEP, 1), lambda i: (i, 0)),
            pl.BlockSpec((STEP, 64, 128), lambda i: (i, 0, 0)),
            full((128, 256)),
            full((128, 256)),
        ],
        out_specs=full((16, 128 // share, 256)),
        out_shape=jax.ShapeDtypeStruct((16, 128 // share, 256), BF16),
        scratch_shapes=[pltpu.VMEM((128, 256), F32)],
        compiler_params=pltpu.CompilerParams(vmem_limit_bytes=32 * 2**20),
        name="warp_forward",
    )(columns, weights, prior, current)


def warp_adjoint(share, columns, rows, weights, parts):
    return pl.pallas_call(
        functools.partial(adjoint_kernel, share),
        grid=(256 // STEP,),
        in_specs=[
            pl.BlockSpec((8 * STEP, 1), lambda i: (i, 0)),
            pl.BlockSpec((1, 8 * STEP), lambda i: (0, i)),
            pl.BlockSpec((STEP, 64, 128), lambda i: (i, 0, 0)),
            full((16, 128 // share, 256)),
        ],
        out_specs=[full((128, 256)), full((128, 256))],
        out_shape=[jax.ShapeDtypeStruct((128, 256), F32), jax.ShapeDtypeStruct((128, 256), BF16)],
        scratch_shapes=[pltpu.VMEM((128, 256), BF16), pltpu.VMEM((128, 256), F32)],
        compiler_params=pltpu.CompilerParams(vmem_limit_bytes=32 * 2**20),
        name="warp_adjoint",
    )(columns, rows, weights, parts)


def data_gradient(share, moved, sens, measured, mask):
    depths, coils = Z // share, 2 * share
    matrix = row_matrix()
    return pl.pallas_call(
        data_kernel,
        grid=(depths, coils // PAIR),
        in_specs=[
            pl.BlockSpec((16, 1, 16, 256), lambda z, c: (0, z, 0, 0)),
            pl.BlockSpec((16, PAIR, 1, 16, 256), lambda z, c: (0, c, z, 0, 0)),
            pl.BlockSpec((PAIR, 1, NY, 256), lambda z, c: (c, z, 0, 0)),
            full((NY, NX)),
            full((256, 256)),
            full((256, 256)),
            full((NY, 2 * NY)),
        ],
        out_specs=pl.BlockSpec((16, 1, 16, 256), lambda z, c: (0, z, 0, 0)),
        out_shape=jax.ShapeDtypeStruct((16, depths, 16, 256), BF16),
        scratch_shapes=[pltpu.VMEM((NY, 256), F32)],
        compiler_params=pltpu.CompilerParams(vmem_limit_bytes=32 * 2**20),
        name="data_gradient",
    )(moved, sens, measured, mask, jnp.asarray(matrix), jnp.asarray(matrix.T), jnp.asarray(column_table()))


def on_device(share, cine_image, warp_blocks, warp_index, sample_mask, kspace_data, sensitivity):
    coil = ("group", "member")
    groups, depths = 16 // share, Z // share
    loop = 16
    forward = [(i, (i + 1) % loop) for i in range(loop)]
    backward = [((i + 1) % loop, i) for i in range(loop)]
    current = cine_image.reshape(128, 256)
    prior = lax.ppermute(current, "bin", forward)

    measured = kspace_data[0].reshape(2, NY, share, depths, 256).transpose(2, 0, 3, 1, 4)
    if share > 1:
        measured = lax.all_to_all(measured, "member", 0, 0, tiled=True)
    measured = measured.reshape(2 * share, depths, NY, 256)
    sens = sensitivity.reshape(groups, 2 * share, 16, share, depths, 256).transpose(0, 3, 1, 4, 2, 5)
    sens = sens.reshape(16, 2 * share, depths, 16, 256)
    sens = lax.all_to_all(sens, coil, 0, 0, tiled=True)

    weights = warp_blocks.reshape(256, 2, 32, 128).transpose(0, 2, 1, 3).reshape(256, 64, 128)
    index = warp_index[0] - lax.axis_index(coil) * 256
    index = jnp.broadcast_to(index[:, :, None], (256, 2, 4)).reshape(2048)
    moved = warp_forward(share, index.reshape(2048, 1), weights, prior, current)
    moved = lax.all_to_all(moved, coil, 0, 0, tiled=True).reshape(16, depths, 16, 256)
    parts = data_gradient(share, moved, sens, measured, sample_mask[0])
    parts = lax.all_to_all(parts, coil, 0, 0, tiled=True).reshape(16, 128 // share, 256)
    grad, pulled = warp_adjoint(share, index.reshape(2048, 1), index.reshape(1, 2048), weights, parts)
    from_next = lax.ppermute(pulled, "bin", backward)
    return (grad + from_next.astype(F32)).reshape(1, 16, Z, 256)


def solution(mesh):
    share = SHARE
    inner = Mesh(mesh.devices.reshape(16, 16 // share, share), ("bin", "group", "member"))
    coil = ("group", "member")
    return jax.shard_map(
        functools.partial(on_device, share),
        mesh=inner,
        in_specs=(
            P("bin", coil, None, None),
            P("bin", coil, None, None),
            P("bin", coil, None),
            P("bin", None, None),
            P("bin", coil, None, None, None),
            P(None, coil, None, None),
        ),
        out_specs=P("bin", coil, None, None),
        check_vma=False,
    )
```

time: 243 us -> 159 us (0.65)
  waiting for transfers between devices: 126 us -> 34.9 us
  blocking collectives: 0 us -> 52.8 us
  local copies, waits for them, and re-layouts: 45.4 us -> 20.3 us
  Pallas kernels: 0 us -> 24.2 us
  matrix products: 20.8 us -> 0 us
  between operations: 13.7 us -> 0.11 us
  other arithmetic: 10.4 us -> 1.35 us
    reduce_scatter x1 -> x0, waiting for transfers between devices: 71.2 us -> none  [on_device(): lax.psum_scatter(conj_sum(sens_rows, row_apply(back_columns, row_matrix,...]
    all_to_all x0 -> x1, blocking collectives: none -> 52.8 us  [on_device(): sens = lax.all_to_all(sens, coil, 0, 0, tiled=True)]
    all_gather x1 -> x0, waiting for transfers between devices: 51 us -> none  [on_device(): lax.all_gather(moved_image, 'coil', axis=0, tiled=True)]
    all_to_all x1 -> x3, waiting for transfers between devices: 0.01 us -> 30 us  [the longest x1 16.6 us: on_device(): measured = lax.all_to_all(measured, 'member', 0, 0, tiled=True)]
    pallas_call x0 -> x3, Pallas kernels: none -> 24.2 us  [the longest x1 8.82 us: warp_forward(): pl.pallas_call(functools.partial(warp_kernel, share), grid=(256 // STEP,)...]
    dot_general x6 -> x0, matrix products: 20.8 us -> none  [the longest x2 7.98 us: column_transform(): jnp.einsum('tky,cyzx->tckzx', tables, values, preferred_element_type=jnp....]
    unnamed x28 -> x18, local copies, waits for them, and re-layouts: 19.6 us -> 5.92 us
    ppermute x2, starting transfers between devices: 14.9 us -> 7.74 us  [the longest x1 4.13 us: on_device(): prior = lax.ppermute(current, 'bin', forward)]
  transfers between devices with their start and end apart: 5 -> 5, of which waited for: 3 -> 4; matrix products, arithmetic and copies ran while one was open for 19% -> 10% of each run, Pallas kernels for 0% -> 0%
where the time goes in v1:
time: 159 us; the launch traced here: 158 us
  blocking collectives  52.8 us (33%)
  waiting for transfers between devices  34.9 us (22%)
  starting transfers between devices  24.3 us (15%)
  Pallas kernels  24.2 us (15%)
  local copies, waits for them, and re-layouts  20.3 us (13%)
    all_to_all x1, blocking collectives, on_device(): sens = lax.all_to_all(sens, coil, 0, 0, tiled=True)  52.8 us
    all_to_all x1, waiting for transfers between devices, on_device(): measured = lax.all_to_all(measured, 'member', 0, 0, tiled=True)  16.6 us
    pallas_call x1, Pallas kernels, warp_forward(): pl.pallas_call(functools.partial(warp_kernel, share), grid=(256 // STEP,)...  8.82 us
    all_to_all x1, starting transfers between devices, on_device(): lax.all_to_all(moved, coil, 0, 0, tiled=True).reshape(16, depths, 16, 256)  8.32 us
    all_to_all x1, waiting for transfers between devices, on_device(): lax.all_to_all(parts, coil, 0, 0, tiled=True).reshape(16, 128 // share, 256)  8.32 us
    pallas_call x1, Pallas kernels, data_gradient(): pl.pallas_call(data_kernel, grid=(depths, coils // PAIR), in_specs=[pl.Bl...  7.95 us
    reshape x2, local copies, waits for them, and re-layouts, on_device(): sensitivity.reshape(groups, 2 * share, 16, share, depths, 256)  7.66 us
    pallas_call x1, Pallas kernels, warp_adjoint(): pl.pallas_call(functools.partial(adjoint_kernel, share), grid=(256 // STE...  7.46 us
  transfers between devices with their start and end apart: 5, of which 4 were waited for; matrix products, arithmetic and copies ran while one was open for 10% of the time, Pallas kernels for 0%

profile of v1, /device:TPU:1, one launch (start us, length us, event | category | flops | bytes accessed | tf_op | source)
XLA Modules:
  0.0 158.0 jit_solution(14268778072207960744)
XLA Ops:
  0.0 4.1 %collective-permute-start = (bf16[128,256]{1,0:T(8,128)(2,1)}, bf16[128,256]{1,0:T(8,128)(2,1)S(1)}, u32[]{:S(2)}, u32[]{:S(2)}) collective-permute-start(bf16[128,256]{1,0:T(8,128)(2,1)} %bitcast.30), channel_id=1, source_target_pairs={{0,16},{16,32},{32,48},{48,64},{64,80},{80,96},{96,112},{112,128},... | collective-permute-start | bytes 196616 | tf_op jit(solution)/shard_map/ppermute | solution.py:268
  4.1 0.7 subtract_bitcast_fusion
  4.8 0.1 copy.14
  5.0 0.3 broadcast_in_dim.2
  5.3 0.0 copy-start.8
  5.3 0.4 reshape_reshape.9.col_ref
  5.8 0.0 collective-permute-done.prior_ref
  5.8 2.2 %copy-done = bf16[1,256,2,4096]{3,2,1,0:T(2,128)(2,1)S(1)} copy-done((bf16[1,256,2,4096]{3,2,1,0:T(2,128)(2,1)S(1)}, bf16[1,256,2,4096]{3,2,1,0:T(2,128)(2,1)}, u32[]{:S(2)}) %copy-start) | copy-done | bytes 4194328
  8.0 0.8 copy-done.7
  8.8 8.8 %warp_forward.1 = bf16[16,32,256]{2,1,0:T(8,128)(2,1)} custom-call(s32[2048,1]{1,0:T(8,128)S(1)} %reshape_reshape.9.col_ref, bf16[256,64,128]{2,1,0:T(8,128)(2,1)S(1)} %bitcast.24, bf16[128,256]{1,0:T(8,128)(2,1)S(1)} %collective-permute-done.prior_ref, bf16[128,256]{1,0:T(8,128)(2,1)S(1)} %bitcast.31), custom_call_target="tpu_custom_call" | custom-call | tf_op jit(solution)/shard_map/warp_forward/pallas_call | solution.py:203
  17.6 0.0 copy-done.8
  17.6 8.3 %all-to-all-start = ((bf16[16,32,256]{2,1,0:T(8,128)(2,1)}), bf16[16,32,256]{2,1,0:T(8,128)(2,1)S(1)}, u32[]{:S(2)}, u32[]{:S(2)}) async-start(bf16[16,32,256]{2,1,0:T(8,128)(2,1)} %warp_forward.1), calls=%async_computation | async-start | bytes 524288 | tf_op jit(solution)/shard_map/all_to_all | solution.py:282
  26.0 2.8 %reshape_squeeze.3 = bf16[2,256,4,2,256]{4,3,2,1,0:T(2,128)(2,1)S(1)} reshape(bf16[1,2,256,8,256]{4,3,2,1,0:T(8,128)(2,1)} %param.13) | data formatting | bytes 4194304 | tf_op jit(solution)/shard_map/reshape;squeeze | solution.py:270
  28.7 1.8 %copy.21 = bf16[2,256,4,2,256]{4,1,3,0,2:T(8,128)(2,1)} copy(bf16[2,256,4,2,256]{4,3,2,1,0:T(2,128)(2,1)S(1)} %reshape_squeeze.3) | data formatting | bytes 4194304 | tf_op jit(solution)/shard_map/reshape;squeeze | solution.py:270
  30.5 5.0 %all-to-all-done = bf16[16,32,256]{2,1,0:T(8,128)(2,1)S(1)} async-done(((bf16[16,32,256]{2,1,0:T(8,128)(2,1)}), bf16[16,32,256]{2,1,0:T(8,128)(2,1)S(1)}, u32[]{:S(2)}, u32[]{:S(2)}) %all-to-all-start) | async-done | bytes 262176 | tf_op jit(solution)/shard_map/all_to_all | solution.py:282
  35.6 3.6 %all-to-all-start.2 = ((bf16[4,2,2,256,256]{4,3,2,1,0:T(8,128)(2,1)}), bf16[4,2,2,256,256]{4,3,2,1,0:T(8,128)(2,1)S(1)}, u32[]{:S(2)}, u32[]{:S(2)}) async-start(bf16[4,2,2,256,256]{4,3,2,1,0:T(8,128)(2,1)} %bitcast.32), calls=%async_computation.2 | async-start | bytes 4194304 | tf_op jit(solution)/shard_map/all_to_all | solution.py:272
  39.2 4.1 %reshape.38 = bf16[4,8,16,4,2,256]{5,4,3,2,1,0:T(2,128)(2,1)} reshape(bf16[32,16,8,256]{3,2,1,0:T(8,128)(2,1)} %param.14) | data formatting | bytes 4194304 | tf_op jit(solution)/shard_map/reshape | solution.py:274
  43.3 3.5 %copy.17 = bf16[4,8,16,4,2,256]{5,2,4,1,3,0:T(8,128)(2,1)} copy(bf16[4,8,16,4,2,256]{5,4,3,2,1,0:T(2,128)(2,1)} %reshape.38) | data formatting | bytes 4194304 | tf_op jit(solution)/shard_map/reshape | solution.py:274
  46.8 16.6 %all-to-all-done.2 = bf16[4,2,2,256,256]{4,3,2,1,0:T(8,128)(2,1)S(1)} async-done(((bf16[4,2,2,256,256]{4,3,2,1,0:T(8,128)(2,1)}), bf16[4,2,2,256,256]{4,3,2,1,0:T(8,128)(2,1)S(1)}, u32[]{:S(2)}, u32[]{:S(2)}) %all-to-all-start.2) | async-done | bytes 2097184 | tf_op jit(solution)/shard_map/all_to_all | solution.py:272
  63.5 52.8 %all_to_all.20.sens_ref = bf16[16,8,2,16,256]{4,3,2,1,0:T(8,128)(2,1)S(1)} all-to-all(bf16[16,8,2,16,256]{4,3,2,1,0:T(8,128)(2,1)} %bitcast.33), channel_id=1, replica_groups=mesh['bin'=16,'group'=4,'member'=4] {'group','member'}, dimensions={0} | all-to-all | bytes 4194304 | tf_op jit(solution)/shard_map/all_to_all | solution.py:276
  116.2 0.0 copy-done.3
  116.2 0.0 copy-done.6
  116.3 7.9 %data_gradient.1 = bf16[16,2,16,256]{3,2,1,0:T(8,128)(2,1)S(1)} custom-call(bf16[16,2,16,256]{3,2,1,0:T(8,128)(2,1)S(1)} %bitcast.27, bf16[16,8,2,16,256]{4,3,2,1,0:T(8,128)(2,1)S(1)} %all_to_all.20.sens_ref, bf16[8,2,256,256]{3,2,1,0:T(8,128)(2,1)S(1)} %bitcast.26, s32[256,128]{1,0:T(8,128)S(1)} %bitcast.29, bf16[256,256]{1,0:T(8,128)(2,1)S(1)} %copy-done.6, ...), custom_call_target="tpu_custom_call" | custom-call | tf_op jit(solution)/shard_map/data_gradient/pallas_call | solution.py:241
  124.2 0.7 copy-done.2
  124.9 4.6 %all-to-all-start.3 = ((bf16[16,2,16,256]{3,2,1,0:T(8,128)(2,1)}), bf16[16,2,16,256]{3,2,1,0:T(8,128)(2,1)S(1)}, u32[]{:S(2)}, u32[]{:S(2)}) async-start(bf16[16,2,16,256]{3,2,1,0:T(8,128)(2,1)} %copy-done.2), calls=%async_computation.3 | async-start | bytes 524288 | tf_op jit(solution)/shard_map/all_to_all | solution.py:284
  129.5 1.3 reshape_reshape.8.row_ref
  130.8 8.3 %all-to-all-done.3 = bf16[16,2,16,256]{3,2,1,0:T(8,128)(2,1)S(1)} async-done(((bf16[16,2,16,256]{3,2,1,0:T(8,128)(2,1)}), bf16[16,2,16,256]{3,2,1,0:T(8,128)(2,1)S(1)}, u32[]{:S(2)}, u32[]{:S(2)}) %all-to-all-start.3) | async-done | bytes 262176 | tf_op jit(solution)/shard_map/all_to_all | solution.py:284
  139.1 2.2 %copy-done.1 = bf16[1,256,2,4096]{3,2,1,0:T(2,128)(2,1)S(1)} copy-done((bf16[1,256,2,4096]{3,2,1,0:T(2,128)(2,1)S(1)}, bf16[1,256,2,4096]{3,2,1,0:T(2,128)(2,1)}, u32[]{:S(2)}) %copy-start.1) | copy-done | bytes 4194328
  141.3 7.5 %warp_adjoint.1 = (f32[128,256]{1,0:T(8,128)S(1)}, bf16[128,256]{1,0:T(8,128)(2,1)S(1)}) custom-call(s32[2048,1]{1,0:T(8,128)S(1)} %reshape_reshape.9.col_ref, s32[1,2048]{1,0:T(1,128)S(1)} %reshape_reshape.8.row_ref, bf16[256,64,128]{2,1,0:T(8,128)(2,1)S(1)} %bitcast.25, bf16[16,32,256]{2,1,0:T(8,128)(2,1)S(1)} %bitcast.28), custom_call_target="tpu_custom_call" | custom-call | tf_op jit(solution)/shard_map/warp_adjoint/pallas_call | solution.py:221
  148.8 3.6 %collective-permute-start.1 = (bf16[128,256]{1,0:T(8,128)(2,1)S(1)}, bf16[128,256]{1,0:T(8,128)(2,1)S(1)}, u32[]{:S(2)}, u32[]{:S(2)}) collective-permute-start(bf16[128,256]{1,0:T(8,128)(2,1)S(1)} %get-tuple-element.8), channel_id=1, source_target_pairs={{16,0},{32,16},{48,32},{64,48},{80,64},{96,80},{112,96},{128,112},... | collective-permute-start | bytes 196616 | tf_op jit(solution)/shard_map/ppermute | solution.py:286
  152.4 4.9 %collective-permute-done.1 = bf16[128,256]{1,0:T(8,128)(2,1)S(1)} collective-permute-done((bf16[128,256]{1,0:T(8,128)(2,1)S(1)}, bf16[128,256]{1,0:T(8,128)(2,1)S(1)}, u32[]{:S(2)}, u32[]{:S(2)}) %collective-permute-start.1) | collective-permute-done | bytes 65568 | tf_op jit(solution)/shard_map/ppermute | solution.py:286
  157.3 0.7 add_bitcast_fusion
  (10 shorter events, 0.0 us)
Async XLA Ops:
  0.0 5.8 %collective-permute-start = (bf16[128,256]{1,0:T(8,128)(2,1)}, bf16[128,256]{1,0:T(8,128)(2,1)S(1)}, u32[]{:S(2)}, u32[]{:S(2)}) collective-permute-start(bf16[128,256]{1,0:T(8,128)(2,1)} %bitcast.30), channel_id=1, source_target_pairs={{0,16},{16,32},{32,48},{48,64},{64,80},{80,96},{96,112},{112,128},... | collective-permute-start | bytes 196616 | tf_op jit(solution)/shard_map/ppermute | solution.py:268
  5.3 12.3 %copy-start.8 = (s32[256,2,4]{2,1,0:T(2,128)}, s32[256,2,4]{2,1,0:T(2,128)S(1)}, u32[]{:S(2)}) copy-start(s32[256,2,4]{2,1,0:T(2,128)S(1)} %broadcast_in_dim.2) | copy-start | bytes 24580
  5.8 2.2 %copy-start = (bf16[1,256,2,4096]{3,2,1,0:T(2,128)(2,1)S(1)}, bf16[1,256,2,4096]{3,2,1,0:T(2,128)(2,1)}, u32[]{:S(2)}) copy-start(bf16[1,256,2,4096]{3,2,1,0:T(2,128)(2,1)} %param.10) | copy-start | bytes 12582916
  8.0 0.8 copy-start.7
  17.6 17.9 %all-to-all-start = ((bf16[16,32,256]{2,1,0:T(8,128)(2,1)}), bf16[16,32,256]{2,1,0:T(8,128)(2,1)S(1)}, u32[]{:S(2)}, u32[]{:S(2)}) async-start(bf16[16,32,256]{2,1,0:T(8,128)(2,1)} %warp_forward.1), calls=%async_computation | async-start | bytes 524288 | tf_op jit(solution)/shard_map/all_to_all | solution.py:282
  35.6 27.9 %all-to-all-start.2 = ((bf16[4,2,2,256,256]{4,3,2,1,0:T(8,128)(2,1)}), bf16[4,2,2,256,256]{4,3,2,1,0:T(8,128)(2,1)S(1)}, u32[]{:S(2)}, u32[]{:S(2)}) async-start(bf16[4,2,2,256,256]{4,3,2,1,0:T(8,128)(2,1)} %bitcast.32), calls=%async_computation.2 | async-start | bytes 4194304 | tf_op jit(solution)/shard_map/all_to_all | solution.py:272
  63.5 52.8 %copy-start.3 = (bf16[256,512]{1,0:T(8,128)(2,1)S(1)}, bf16[256,512]{1,0:T(8,128)(2,1)}, u32[]{:S(2)}) copy-start(bf16[256,512]{1,0:T(8,128)(2,1)} %constant.19.clone.table_ref) | copy-start | bytes 786436
  63.5 52.8 %copy-start.4 = (s32[1,256,128]{2,1,0:T(8,128)S(1)}, s32[1,256,128]{2,1,0:T(8,128)}, u32[]{:S(2)}) copy-start(s32[1,256,128]{2,1,0:T(8,128)} %param.12) | copy-start | bytes 393220
  63.5 52.8 %copy-start.5 = (bf16[256,256]{1,0:T(8,128)(2,1)S(1)}, bf16[256,256]{1,0:T(8,128)(2,1)}, u32[]{:S(2)}) copy-start(bf16[256,256]{1,0:T(8,128)(2,1)} %constant.18.clone.back_ref) | copy-start | bytes 393220
  63.5 52.8 %copy-start.6 = (bf16[256,256]{1,0:T(8,128)(2,1)S(1)}, bf16[256,256]{1,0:T(8,128)(2,1)}, u32[]{:S(2)}) copy-start(bf16[256,256]{1,0:T(8,128)(2,1)} %constant.17.clone.row_ref) | copy-start | bytes 393220
  124.2 0.7 copy-start.2
  124.9 14.2 %all-to-all-start.3 = ((bf16[16,2,16,256]{3,2,1,0:T(8,128)(2,1)}), bf16[16,2,16,256]{3,2,1,0:T(8,128)(2,1)S(1)}, u32[]{:S(2)}, u32[]{:S(2)}) async-start(bf16[16,2,16,256]{3,2,1,0:T(8,128)(2,1)} %copy-done.2), calls=%async_computation.3 | async-start | bytes 524288 | tf_op jit(solution)/shard_map/all_to_all | solution.py:284
  139.1 2.2 %copy-start.1 = (bf16[1,256,2,4096]{3,2,1,0:T(2,128)(2,1)S(1)}, bf16[1,256,2,4096]{3,2,1,0:T(2,128)(2,1)}, u32[]{:S(2)}) copy-start(bf16[1,256,2,4096]{3,2,1,0:T(2,128)(2,1)} %param.10) | copy-start | bytes 12582916
  148.8 8.5 %collective-permute-start.1 = (bf16[128,256]{1,0:T(8,128)(2,1)S(1)}, bf16[128,256]{1,0:T(8,128)(2,1)S(1)}, u32[]{:S(2)}, u32[]{:S(2)}) collective-permute-start(bf16[128,256]{1,0:T(8,128)(2,1)S(1)} %get-tuple-element.8), channel_id=1, source_target_pairs={{16,0},{32,16},{48,32},{64,48},{80,64},{96,80},{112,96},{128,112},... | collective-permute-start | bytes 196616 | tf_op jit(solution)/shard_map/ppermute | solution.py:286

commit v2 on v1

v2 whole, which is shorter than its diff:
```python
import jax
import jax.numpy as jnp
import numpy as np
from jax import lax
from jax.experimental import pallas as pl
from jax.experimental.pallas import tpu as pltpu
from jax.sharding import Mesh
from jax.sharding import PartitionSpec as P

NY = 256
NX = 128
Z = 8
SHARE = 4
PAIR = 4
STEP = 128

VMEM = 60 * 2**20

F32 = jnp.float32
BF16 = jnp.bfloat16


def cosine_sine(length):
    positions = np.arange(length)
    phases = positions[:, None] * positions[None, :] % length
    angles = phases * (2.0 * np.pi / length)
    return np.cos(angles) / np.sqrt(length), np.sin(angles) / np.sqrt(length)


def row_matrix():
    cosine, sine = cosine_sine(NX)
    return np.block([[cosine, -sine], [sine, cosine]]).astype(BF16)


def column_table():
    return np.concatenate(cosine_sine(NY), axis=1).astype(BF16)


def iota(shape, axis):
    return lax.broadcasted_iota(jnp.int32, shape, axis)


def matmul(a, b):
    return jnp.dot(a, b, preferred_element_type=F32)


def high_low(values):
    high = values.astype(BF16)
    return high, (values - high.astype(F32)).astype(BF16)


def sublane_roles(rows):
    r = iota((rows, 128), 0)
    return r, (r >> 2) & 1, (r >> 1) & 1, r & 1


def shift_lanes(values, distance):
    return jnp.where(
        distance == 1,
        pltpu.roll(values, 1, 1),
        jnp.where(distance == -1, pltpu.roll(values, 127, 1), values),
    )


def as_matrix(condition):
    return condition.astype(F32).astype(BF16)


def depth_major(core):
    to, frm = iota((128, 128), 0), iota((128, 128), 1)
    return as_matrix((to & 15) * Z + ((to >> 4) ^ core) == frm)


def warp_kernel(place_ref, col_ref, w_ref, prior_ref, cur_ref, out_ref, acc_ref):
    step = pl.program_id(0)
    rows = 8 * STEP
    index = col_ref[...]
    r, slot, odd, imag = sublane_roles(rows)
    lane = iota((rows, 128), 1)
    half = lane >> 6
    chosen = (lane == (index >> 1)).astype(F32).astype(BF16)
    both = matmul(chosen, prior_ref[...])
    v = jnp.where(imag == 1, both[:, 128:], both[:, :128])
    v = jnp.where((index & 1) == odd, v, pltpu.roll(v, 64, 1))
    v = jnp.where(half == odd, v, 0.0)
    f = lax.dot_general(
        v.reshape(STEP // 4, 32, 128).astype(BF16),
        w_ref[...].reshape(STEP // 4, 256, 128),
        (((2,), (2,)), ((0,), (0,))),
        preferred_element_type=F32,
    ).reshape(rows, 256)
    f = jnp.where(((r >> 4) & 1) == 0, f[:, :128], f[:, 128:])
    f = jnp.where(((lane & 1) == slot) & (half == ((r >> 3) & 1)), f, 0.0)
    f = shift_lanes(f, odd - slot)
    f = jnp.concatenate([jnp.where(imag == 0, f, 0.0), jnp.where(imag == 1, f, 0.0)], axis=1)
    lines = STEP // 2
    gather = as_matrix(iota((lines, rows), 1) >> 4 == iota((lines, rows), 0))
    high, low = high_low(f)
    acc_ref[pl.ds(pl.multiple_of(step * lines, lines), lines), :] = matmul(gather, high) + matmul(gather, low)

    @pl.when(step == pl.num_programs(0) - 1)
    def _():
        moved = (cur_ref[...].astype(F32) + acc_ref[...]).astype(BF16)
        turned = matmul(depth_major(place_ref[1]), moved).astype(BF16).reshape(SHARE, 128 // SHARE, 256)
        for g in range(16 // SHARE):
            out_ref[g * SHARE : (g + 1) * SHARE] = turned


def adjoint_kernel(place_ref, col_ref, row_ref, w_ref, parts_ref, grad_ref, pulled_ref, image_ref, acc_ref):
    step = pl.program_id(0)
    rows = 8 * STEP

    @pl.when(step == 0)
    def _():
        total = parts_ref[0:SHARE].astype(F32)
        for g in range(1, 16 // SHARE):
            total = total + parts_ref[g * SHARE : (g + 1) * SHARE].astype(F32)
        total = total.reshape(128, 256)
        frm, to = iota((128, 128), 1), iota((128, 128), 0)
        turn = as_matrix((frm & 15) * Z + ((frm >> 4) ^ place_ref[1]) == to)
        high, low = high_low(total)
        lowest = (total - high.astype(F32) - low.astype(F32)).astype(BF16)
        grad = matmul(turn, high) + matmul(turn, low) + matmul(turn, lowest)
        grad_ref[...] = grad
        image_ref[...] = grad.astype(BF16)
        acc_ref[...] = jnp.zeros_like(acc_ref)

    index = col_ref[...]
    r, slot, odd, imag = sublane_roles(rows)
    lane = iota((rows, 128), 1)
    half = lane >> 6
    chosen = (lane == step * (STEP // 2) + (r >> 4)).astype(F32).astype(BF16)
    both = matmul(chosen, image_ref[...])
    v = jnp.where(imag == 1, both[:, 128:], both[:, :128])
    v = jnp.where(half == ((r >> 3) & 1), v, pltpu.roll(v, 64, 1))
    v = jnp.where((lane & 1) == odd, v, 0.0)
    v = shift_lanes(v, slot - odd)
    place4 = (r >> 3) & 3
    v = jnp.concatenate([jnp.where(half == place4, v, 0.0), jnp.where(half + 2 == place4, v, 0.0)], axis=1)
    f = lax.dot_general(
        v.reshape(STEP // 4, 32, 256).astype(BF16),
        w_ref[...].reshape(STEP // 4, 256, 128),
        (((2,), (1,)), ((0,), (0,))),
        preferred_element_type=F32,
    ).reshape(rows, 128)
    f = jnp.where(half == odd, f, 0.0)
    f = f + pltpu.roll(f, 64, 1)
    f = jnp.where(half == (index & 1), f, 0.0)
    f = jnp.concatenate([jnp.where(imag == 0, f, 0.0), jnp.where(imag == 1, f, 0.0)], axis=1)
    scatter = (iota((128, rows), 0) == (row_ref[...] >> 1)).astype(F32).astype(BF16)
    high, low = high_low(f)
    acc_ref[...] += matmul(scatter, high) + matmul(scatter, low)

    @pl.when(step == pl.num_programs(0) - 1)
    def _():
        pulled_ref[...] = acc_ref[...].astype(BF16)


def data_kernel(
    place_ref,
    moved_ref,
    own_ref,
    other_ref,
    data0_ref,
    data1_ref,
    data2_ref,
    data3_ref,
    mask_ref,
    row_ref,
    back_ref,
    table_ref,
    out_ref,
    acc_ref,
):
    depth, chunk = pl.program_id(0), pl.program_id(1)
    moved = moved_ref[...].reshape(NY, 256).astype(F32)
    image_re, image_im = moved[:, :NX], moved[:, NX:]
    mask = mask_ref[...].astype(F32)
    table = table_ref[...]
    sens_re, sens_im, images = [], [], []
    for c in range(PAIR):
        sens = jnp.where(depth == 0, own_ref[c // 2, :, c % 2], other_ref[c // 2, :, c % 2])
        sens = sens.reshape(NY, 256).astype(F32)
        sens_re.append(sens[:, :NX])
        sens_im.append(sens[:, NX:])
        re = sens_re[c] * image_re - sens_im[c] * image_im
        im = sens_re[c] * image_im + sens_im[c] * image_re
        images.append(jnp.concatenate([re, im], axis=1).astype(BF16))
    spectra = matmul(jnp.concatenate(images, axis=0), row_ref[...])
    tops, bottoms = [], []
    for c in range(PAIR):
        s = spectra[c * NY : (c + 1) * NY]
        tops.append(s)
        bottoms += [s[:, NX:], -s[:, :NX]]
    stacked = jnp.concatenate([jnp.concatenate(tops, axis=1), jnp.concatenate(bottoms, axis=1)], axis=0).astype(BF16)
    spectra = matmul(table, stacked)
    tops, bottoms = [], []
    for c in range(PAIR):
        source = place_ref[3 + chunk * (PAIR // 2) + c // 2]
        low = jnp.where(source == 0, data0_ref[c % 2, 0], data1_ref[c % 2, 0])
        high = jnp.where(source == 2, data2_ref[c % 2, 0], data3_ref[c % 2, 0])
        measured = jnp.where(source < 2, low, high).astype(F32)
        s = spectra[:, c * 256 : (c + 1) * 256] - measured
        res_re, res_im = mask * s[:, :NX], mask * s[:, NX:]
        tops += [res_re, res_im]
        bottoms += [-res_im, res_re]
    stacked = jnp.concatenate([jnp.concatenate(tops, axis=1), jnp.concatenate(bottoms, axis=1)], axis=0).astype(BF16)
    columns = matmul(table, stacked).astype(BF16)
    rows = jnp.concatenate([columns[:, c * 256 : (c + 1) * 256] for c in range(PAIR)], axis=0)
    rows = matmul(rows, back_ref[...])
    real = imag = 0.0
    for c in range(PAIR):
        b = rows[c * NY : (c + 1) * NY]
        back_re, back_im = b[:, :NX], b[:, NX:]
        real += sens_re[c] * back_re + sens_im[c] * back_im
        imag += sens_re[c] * back_im - sens_im[c] * back_re
    both = jnp.concatenate([real, imag], axis=1)
    total = jnp.where(chunk == 0, both, acc_ref[...] + both)
    acc_ref[...] = total
    out_ref[...] = total.astype(BF16).reshape(out_ref.shape)


def pick_kernel(place_ref, sens_ref, out_ref):
    to, frm = iota((64, 128), 0), iota((64, 128), 1)
    turn = as_matrix((to & 15) * Z + (to >> 4) * 2 + place_ref[1] == frm)
    for g in range(16 // SHARE):
        for c in range(2):
            picked = matmul(turn, sens_ref[g, 0, c]).astype(BF16)
            out_ref[g * SHARE : (g + 1) * SHARE, c] = picked.reshape(SHARE, 16, 256)


def turn_kernel(place_ref, data_ref, *out_refs):
    to, frm = iota((128, 128), 0), iota((128, 128), 1)
    depth = (((to >> 5) ^ place_ref[2]) << 1) + (((to >> 4) & 1) ^ place_ref[1])
    turn = as_matrix((to & 15) * Z + depth == frm)
    for b in range(data_ref.shape[1]):
        turned = matmul(turn, data_ref[0, b]).astype(BF16).reshape(SHARE, 2, 16, 256)
        for j in range(SHARE):
            out_refs[j][0, :, b * 16 : (b + 1) * 16] = turned[j]


def full(shape):
    return pl.BlockSpec(shape, lambda *_: (0,) * len(shape))


def call(kernel, place, arrays, grid, in_specs, out_specs, out_shape, scratch, name, micros):
    return pl.pallas_call(
        kernel,
        grid_spec=pltpu.PrefetchScalarGridSpec(
            num_scalar_prefetch=1, grid=grid, in_specs=in_specs, out_specs=out_specs, scratch_shapes=scratch
        ),
        out_shape=out_shape,
        compiler_params=pltpu.CompilerParams(vmem_limit_bytes=VMEM),
        cost_estimate=pl.CostEstimate(flops=0, bytes_accessed=int(micros * 3e6), transcendentals=0),
        name=name,
    )(place, *arrays)


def warp_forward(place, columns, weights, prior, current):
    shape = (16, 128 // SHARE, 256)
    return call(
        warp_kernel,
        place,
        (columns, weights, prior, current),
        (256 // STEP,),
        [
            pl.BlockSpec((8 * STEP, 1), lambda i, p: (i, 0)),
            pl.BlockSpec((STEP, 64, 128), lambda i, p: (i, 0, 0)),
            full((128, 256)),
            full((128, 256)),
        ],
        full(shape),
        jax.ShapeDtypeStruct(shape, BF16),
        [pltpu.VMEM((128, 256), F32)],
        "warp_forward",
        8,
    )


def warp_adjoint(place, columns, rows, weights, parts):
    return call(
        adjoint_kernel,
        place,
        (columns, rows, weights, parts),
        (256 // STEP,),
        [
            pl.BlockSpec((8 * STEP, 1), lambda i, p: (i, 0)),
            pl.BlockSpec((1, 8 * STEP), lambda i, p: (0, i)),
            pl.BlockSpec((STEP, 64, 128), lambda i, p: (i, 0, 0)),
            full((16, 128 // SHARE, 256)),
        ],
        [full((128, 256)), full((128, 256))],
        [jax.ShapeDtypeStruct((128, 256), F32), jax.ShapeDtypeStruct((128, 256), BF16)],
        [pltpu.VMEM((128, 256), BF16), pltpu.VMEM((128, 256), F32)],
        "warp_adjoint",
        8,
    )


def data_gradient(place, moved, own, other, measured, mask):
    matrix = row_matrix()
    last = 8 // PAIR - 1
    sens_block = (PAIR // 2, 16, 2, 16, 256)
    return call(
        data_kernel,
        place,
        (moved, own, other, *measured, mask, jnp.asarray(matrix), jnp.asarray(matrix.T), jnp.asarray(column_table())),
        (2, 8 // PAIR),
        [
            pl.BlockSpec((16, 1, 16, 256), lambda z, c, p: (0, z, 0, 0)),
            pl.BlockSpec(sens_block, lambda z, c, p: (jnp.where(z == 0, c, last), 0, 0, 0, 0)),
            pl.BlockSpec(sens_block, lambda z, c, p: (jnp.where(z == 0, 0, c), 0, 0, 0, 0)),
            *[pl.BlockSpec((2, 1, NY, 256), lambda z, c, p: (0, z, 0, 0))] * 4,
            full((NY, NX)),
            full((256, 256)),
            full((256, 256)),
            full((NY, 2 * NY)),
        ],
        pl.BlockSpec((16, 1, 16, 256), lambda z, c, p: (0, z, 0, 0)),
        jax.ShapeDtypeStruct((16, 2, 16, 256), BF16),
        [pltpu.VMEM((NY, 256), F32)],
        "data_gradient",
        8,
    )


def pick_share(place, sensitivity):
    return call(
        pick_kernel,
        place,
        (sensitivity.reshape(4, 4, 2, 128, 256),),
        (1,),
        [pl.BlockSpec((4, 1, 2, 128, 256), lambda g, p: (0, p[0], 0, 0, 0))],
        full((16, 2, 16, 256)),
        jax.ShapeDtypeStruct((16, 2, 16, 256), BF16),
        [],
        "pick_share",
        1,
    )


def turn_data(place, data):
    blocks = 8
    return call(
        turn_kernel,
        place,
        (data.reshape(2, 16, 128, 256),),
        (2, 16 // blocks),
        [pl.BlockSpec((1, blocks, 128, 256), lambda c, b, p: (c, b, 0, 0))],
        [pl.BlockSpec((1, 2, 16 * blocks, 256), lambda c, b, p: (c, 0, b, 0))] * SHARE,
        [jax.ShapeDtypeStruct((2, 2, NY, 256), BF16)] * SHARE,
        [],
        "turn_data",
        3,
    )


def on_device(cine_image, warp_blocks, warp_index, sample_mask, kspace_data, sensitivity):
    loop_axes, coil = ("y", "half", "core"), ("group", "member")
    row, core, member = lax.axis_index("y"), lax.axis_index("core"), lax.axis_index("member")
    offsets = (0, 1, -1, 2)
    place = jnp.stack([row, core, member, *[((row + d) % 4) ^ member for d in offsets]])
    forward = [(i, (i + 1) % 16) for i in range(16)]
    backward = [((i + 1) % 16, i) for i in range(16)]
    current = cine_image.reshape(128, 256)
    prior = lax.ppermute(current, loop_axes, forward)

    sens, prior, kspace_data = lax.optimization_barrier((pick_share(place, sensitivity), prior, kspace_data))
    sens = lax.all_to_all(sens, coil, 0, 0, tiled=True)
    measured = turn_data(place, kspace_data)
    measured = [
        piece if j == 0 else lax.ppermute(piece, "member", [(i, i ^ j) for i in range(SHARE)])
        for j, piece in enumerate(measured)
    ]

    weights = warp_blocks.reshape(256, 2, 32, 128).transpose(0, 2, 1, 3).reshape(256, 64, 128)
    index = warp_index[0] - lax.axis_index(coil) * 256
    index = jnp.broadcast_to(index[:, :, None], (256, 2, 4)).reshape(2048)
    columns, rows = index.reshape(2048, 1), index.reshape(1, 2048)
    prior, sens, measured[0] = lax.optimization_barrier((prior, sens, measured[0]))
    moved = warp_forward(place, columns, weights, prior, current)
    sens = [sens] + [lax.ppermute(sens, "y", [(i, (i - d) % 4) for i in range(4)]) for d in offsets[1:]]
    moved, sens, measured[1], measured[2] = lax.optimization_barrier((moved, sens, measured[1], measured[2]))
    moved = lax.all_to_all(moved, coil, 0, 0, tiled=True).reshape(16, 2, 16, 256)
    sens = jnp.stack(sens)
    other = lax.ppermute(sens, "core", [(0, 1), (1, 0)])
    parts = data_gradient(place, moved, sens, other, measured, sample_mask[0])
    parts = lax.all_to_all(parts, coil, 0, 0, tiled=True).reshape(16, 32, 256)
    grad, pulled = warp_adjoint(place, columns, rows, weights, parts)
    from_next = lax.ppermute(pulled, loop_axes, backward)
    return (grad + from_next.astype(F32)).reshape(1, 16, Z, 256)


def solution(mesh):
    inner = Mesh(mesh.devices.reshape(4, 2, 2, 16 // SHARE, SHARE), ("y", "half", "core", "group", "member"))
    bins, coil = ("y", "half", "core"), ("group", "member")
    return jax.shard_map(
        on_device,
        mesh=inner,
        in_specs=(
            P(bins, coil, None, None),
            P(bins, coil, None, None),
            P(bins, coil, None),
            P(bins, None, None),
            P(bins, coil, None, None, None),
            P(None, coil, None, None),
        ),
        out_specs=P(bins, coil, None, None),
        check_vma=False,
    )
```

time: 159 us -> 106 us (0.67)
  blocking collectives: 52.8 us -> 0 us
  local copies, waits for them, and re-layouts: 20.3 us -> 6.04 us
  starting transfers between devices: 24.3 us -> 37.3 us
  Pallas kernels: 24.2 us -> 29.1 us
  waiting for transfers between devices: 34.9 us -> 31.4 us
    all_to_all x1 -> x0, blocking collectives: 52.8 us -> none  [on_device(): sens = lax.all_to_all(sens, coil, 0, 0, tiled=True)]
    all_to_all x3, waiting for transfers between devices: 30 us -> 14.7 us  [the longest x1 8.8 us: on_device(): parts = lax.all_to_all(parts, coil, 0, 0, tiled=True).reshape(16, 32, 256)]
    ppermute x2 -> x9, starting transfers between devices: 7.74 us -> 20.2 us  [the longest x3 5.85 us: on_device(): lax.ppermute(sens, 'y', [(i, (i - d) % 4) for i in range(4)])]
    ppermute x2 -> x9, waiting for transfers between devices: 4.92 us -> 16.8 us  [the longest x3 12.3 us: on_device(): lax.ppermute(piece, 'member', [(i, i ^ j) for i in range(SHARE)])]
    reshape x2 -> x0, local copies, waits for them, and re-layouts: 7.66 us -> none  [on_device(): sensitivity.reshape(groups, 2 * share, 16, share, depths, 256)]
    pallas_call x3 -> x5, Pallas kernels: 24.2 us -> 29.1 us  [call(): pl.pallas_call(kernel, grid_spec=pltpu.PrefetchScalarGridSpec(num_scalar_...]
    unnamed x18 -> x16, local copies, waits for them, and re-layouts: 5.92 us -> 2.57 us
    another operation x4 -> x3, local copies, waits for them, and re-layouts: 6.3 us -> 3 us  [the longest x2 2.39 us: on_device(): columns, rows = (index.reshape(2048, 1), index.reshape(1, 2048))]
  transfers between devices with their start and end apart: 5 -> 12, of which waited for: 4 -> 5; matrix products, arithmetic and copies ran while one was open for 10% -> 3% of each run, Pallas kernels for 0% -> 14%
where the time goes in v2:
time: 106 us
  starting transfers between devices  37.3 us (35%)
  waiting for transfers between devices  31.4 us (30%)
  Pallas kernels  29.1 us (27%)
  local copies, waits for them, and re-layouts  6.04 us (6%)
  other arithmetic  1.71 us (2%)
    pallas_call x5, Pallas kernels, call(): pl.pallas_call(kernel, grid_spec=pltpu.PrefetchScalarGridSpec(num_scalar_...  29.1 us
    ppermute x3, waiting for transfers between devices, on_device(): lax.ppermute(piece, 'member', [(i, i ^ j) for i in range(SHARE)])  12.3 us
    all_to_all x1, waiting for transfers between devices, on_device(): parts = lax.all_to_all(parts, coil, 0, 0, tiled=True).reshape(16, 32, 256)  8.8 us
    all_to_all x1, starting transfers between devices, on_device(): sens = lax.all_to_all(sens, coil, 0, 0, tiled=True)  8.32 us
    ppermute x3, starting transfers between devices, on_device(): lax.ppermute(sens, 'y', [(i, (i - d) % 4) for i in range(4)])  5.85 us
    all_to_all x1, starting transfers between devices, on_device(): parts = lax.all_to_all(parts, coil, 0, 0, tiled=True).reshape(16, 32, 256)  4.52 us
    ppermute x1, waiting for transfers between devices, on_device(): from_next = lax.ppermute(pulled, loop_axes, backward)  4.48 us
    ppermute x1, starting transfers between devices, on_device(): other = lax.ppermute(sens, 'core', [(0, 1), (1, 0)])  4.26 us
  transfers between devices with their start and end apart: 12, of which 5 were waited for; matrix products, arithmetic and copies ran while one was open for 3% of the time, Pallas kernels for 14%

profile of v2, /device:TPU:1, one launch (start us, length us, event | category | flops | bytes accessed | tf_op | source)
XLA Modules:
  0.0 105.6 jit_solution(5031139030751249852)
XLA Ops:
  0.0 4.1 %collective-permute-start = (bf16[128,256]{1,0:T(8,128)(2,1)}, bf16[128,256]{1,0:T(8,128)(2,1)S(1)}, u32[]{:S(2)}, u32[]{:S(2)}) collective-permute-start(bf16[128,256]{1,0:T(8,128)(2,1)} %bitcast.37), channel_id=1, source_target_pairs={{0,16},{16,32},{32,48},{48,64},{64,80},{80,96},{96,112},{112,128},... | collective-permute-start | bytes 196616 | tf_op jit(solution)/shard_map/ppermute | solution.py:366
  4.1 0.6 stack.46.place_ref
  4.8 2.8 %pick_share.1 = bf16[16,2,16,256]{3,2,1,0:T(8,128)(2,1)} custom-call(s32[7]{0:T(128)} %stack.46.place_ref, bf16[4,4,2,128,256]{4,3,2,1,0:T(8,128)(2,1)} %bitcast.28), custom_call_target="tpu_custom_call" | custom-call | bytes 3000000 | tf_op jit(solution)/shard_map/pick_share/pallas_call | solution.py:247
  7.5 8.3 %all-to-all-start = ((bf16[16,2,16,256]{3,2,1,0:T(8,128)(2,1)}), bf16[16,2,16,256]{3,2,1,0:T(8,128)(2,1)S(1)}, u32[]{:S(2)}, u32[]{:S(2)}) async-start(bf16[16,2,16,256]{3,2,1,0:T(8,128)(2,1)} %pick_share.1), calls=%async_computation | async-start | bytes 524288 | tf_op jit(solution)/shard_map/all_to_all | solution.py:369
  15.9 5.0 %turn_data.1 = (bf16[2,2,256,256]{3,2,1,0:T(8,128)(2,1)}, bf16[2,2,256,256]{3,2,1,0:T(8,128)(2,1)}, bf16[2,2,256,256]{3,2,1,0:T(8,128)(2,1)}, bf16[2,2,256,256]{3,2,1,0:T(8,128)(2,1)}) custom-call(s32[7]{0:T(128)} %stack.46.place_ref, bf16[2,16,128,256]{3,2,1,0:T(8,128)(2,1)} %bitcast.29), custom_call_target="tpu_custom_call" | custom-call | bytes 9000000 | tf_op jit(solution)/shard_map/turn_data/pallas_call | solution.py:247
  20.8 1.4 %collective-permute-start.4 = (bf16[2,2,256,256]{3,2,1,0:T(8,128)(2,1)}, bf16[2,2,256,256]{3,2,1,0:T(8,128)(2,1)S(1)}, u32[]{:S(2)}, u32[]{:S(2)}) collective-permute-start(bf16[2,2,256,256]{3,2,1,0:T(8,128)(2,1)} %get-tuple-element.30), channel_id=1, source_target_pairs={{0,1},{1,0},{2,3},{3,2},{4,5},{5,4},{6,7},{7,6},{8,9},{9,8},{10,11... | collective-permute-start | bytes 1572872 | tf_op jit(solution)/shard_map/ppermute | solution.py:372
  22.2 1.2 %collective-permute-start.5 = (bf16[2,2,256,256]{3,2,1,0:T(8,128)(2,1)}, bf16[2,2,256,256]{3,2,1,0:T(8,128)(2,1)S(1)}, u32[]{:S(2)}, u32[]{:S(2)}) collective-permute-start(bf16[2,2,256,256]{3,2,1,0:T(8,128)(2,1)} %get-tuple-element.31), channel_id=1, source_target_pairs={{0,2},{1,3},{2,0},{3,1},{4,6},{5,7},{6,4},{7,5},{8,10},{9,11},{10,... | collective-permute-start | bytes 1572872 | tf_op jit(solution)/shard_map/ppermute | solution.py:372
  23.4 2.1 %all-to-all-done = bf16[16,2,16,256]{3,2,1,0:T(8,128)(2,1)S(1)} async-done(((bf16[16,2,16,256]{3,2,1,0:T(8,128)(2,1)}), bf16[16,2,16,256]{3,2,1,0:T(8,128)(2,1)S(1)}, u32[]{:S(2)}, u32[]{:S(2)}) %all-to-all-start) | async-done | bytes 262176 | tf_op jit(solution)/shard_map/all_to_all | solution.py:369
  25.5 3.2 %collective-permute-start.3 = (bf16[16,2,16,256]{3,2,1,0:T(8,128)(2,1)S(1)}, bf16[16,2,16,256]{3,2,1,0:T(8,128)(2,1)S(1)}, u32[]{:S(2)}, u32[]{:S(2)}) collective-permute-start(bf16[16,2,16,256]{3,2,1,0:T(8,128)(2,1)S(1)} %all-to-all-done), channel_id=1, source_target_pairs={{0,128},{64,192},{128,0},{192,64},{1,129},{65,193},{129,1},{193,65... | collective-permute-start | bytes 786440 | tf_op jit(solution)/shard_map/ppermute | solution.py:382
  28.7 0.4 collective-permute-start.2
  29.1 2.3 %collective-permute-start.1 = (bf16[16,2,16,256]{3,2,1,0:T(8,128)(2,1)S(1)}, bf16[16,2,16,256]{3,2,1,0:T(8,128)(2,1)S(1)}, u32[]{:S(2)}, u32[]{:S(2)}) collective-permute-start(bf16[16,2,16,256]{3,2,1,0:T(8,128)(2,1)S(1)} %all-to-all-done), channel_id=1, source_target_pairs={{0,192},{64,0},{128,64},{192,128},{1,193},{65,1},{129,65},{193,129... | collective-permute-start | bytes 786440 | tf_op jit(solution)/shard_map/ppermute | solution.py:382
  31.3 0.1 copy.12
  31.5 0.3 broadcast_in_dim.2
  31.8 1.4 %reshape_reshape.8.col_ref = s32[2048,1]{1,0:T(8,128)} reshape(s32[256,2,4]{2,1,0:T(2,128)S(1)} %broadcast_in_dim.2) | data formatting | bytes 16384 | tf_op jit(solution)/shard_map/reshape;reshape | solution.py:379
  33.3 6.6 %warp_forward.1 = bf16[16,32,256]{2,1,0:T(8,128)(2,1)} custom-call(s32[7]{0:T(128)} %stack.46.place_ref, s32[2048,1]{1,0:T(8,128)} %reshape_reshape.8.col_ref, bf16[256,64,128]{2,1,0:T(8,128)(2,1)} %bitcast.26, bf16[128,256]{1,0:T(8,128)(2,1)} %copy-done.6, bf16[128,256]{1,0:T(8,128)(2,1)} %bitcast.38), custom_call_target="tpu_custom_call" | custom-call | bytes 24000000 | tf_op jit(solution)/shard_map/warp_forward/pallas_call | solution.py:247
  40.0 0.8 copy-done.5
  40.8 0.1 pad_maximum_fusion.own_ref
  40.9 4.3 %collective-permute-start.6 = (bf16[4,16,2,16,256]{4,3,2,1,0:T(8,128)(2,1)S(1)}, bf16[4,16,2,16,256]{4,3,2,1,0:T(8,128)(2,1)S(1)}, u32[]{:S(2)}, u32[]{:S(2)}) collective-permute-start(bf16[4,16,2,16,256]{4,3,2,1,0:T(8,128)(2,1)S(1)} %pad_maximum_fusion.own_ref), channel_id=1, source_target_pairs={{0,16},{16,0},{1,17},{17,1},{2,18},{18,2},{3,19},{19,3},{4,20},{20... | collective-permute-start | bytes 3145736 | tf_op jit(solution)/shard_map/ppermute | solution.py:386
  45.2 4.2 %all-to-all-start.1 = ((bf16[16,32,256]{2,1,0:T(8,128)(2,1)}), bf16[16,32,256]{2,1,0:T(8,128)(2,1)S(1)}, u32[]{:S(2)}, u32[]{:S(2)}) async-start(bf16[16,32,256]{2,1,0:T(8,128)(2,1)} %warp_forward.1), calls=%async_computation.1 | async-start | bytes 524288 | tf_op jit(solution)/shard_map/all_to_all | solution.py:384
  49.5 12.3 %collective-permute-done.7.data3_ref = bf16[2,2,256,256]{3,2,1,0:T(8,128)(2,1)} collective-permute-done((bf16[2,2,256,256]{3,2,1,0:T(8,128)(2,1)}, bf16[2,2,256,256]{3,2,1,0:T(8,128)(2,1)}, u32[]{:S(2)}, u32[]{:S(2)}) %collective-permute-start.7) | collective-permute-done | bytes 524320 | tf_op jit(solution)/shard_map/ppermute | solution.py:372
  61.7 3.8 %all-to-all-done.1 = bf16[16,32,256]{2,1,0:T(8,128)(2,1)S(1)} async-done(((bf16[16,32,256]{2,1,0:T(8,128)(2,1)}), bf16[16,32,256]{2,1,0:T(8,128)(2,1)S(1)}, u32[]{:S(2)}, u32[]{:S(2)}) %all-to-all-start.1) | async-done | bytes 262176 | tf_op jit(solution)/shard_map/all_to_all | solution.py:384
  65.5 0.7 copy-done.1
  66.2 0.4 copy-done.3
  66.6 8.1 %data_gradient.1 = bf16[16,2,16,256]{3,2,1,0:T(8,128)(2,1)} custom-call(s32[7]{0:T(128)} %stack.46.place_ref, bf16[16,2,16,256]{3,2,1,0:T(8,128)(2,1)} %bitcast.30, bf16[4,16,2,16,256]{4,3,2,1,0:T(8,128)(2,1)} %copy-done, bf16[4,16,2,16,256]{4,3,2,1,0:T(8,128)(2,1)} %copy-done.3, bf16[2,2,256,256]{3,2,1,0:T(8,128)(2,1)} %get-tuple-element.37.data0_ref, ...), custom_call_target="tpu_custom_call" | custom-call | bytes 24000000 | tf_op jit(solution)/shard_map/data_gradient/pallas_call | solution.py:247
  74.7 4.5 %all-to-all-start.2 = ((bf16[16,2,16,256]{3,2,1,0:T(8,128)(2,1)}), bf16[16,2,16,256]{3,2,1,0:T(8,128)(2,1)S(1)}, u32[]{:S(2)}, u32[]{:S(2)}) async-start(bf16[16,2,16,256]{3,2,1,0:T(8,128)(2,1)} %data_gradient.1), calls=%async_computation.2 | async-start | bytes 524288 | tf_op jit(solution)/shard_map/all_to_all | solution.py:388
  79.2 0.9 reshape_reshape.7.row_ref
  80.1 8.8 %all-to-all-done.2 = bf16[16,2,16,256]{3,2,1,0:T(8,128)(2,1)S(1)} async-done(((bf16[16,2,16,256]{3,2,1,0:T(8,128)(2,1)}), bf16[16,2,16,256]{3,2,1,0:T(8,128)(2,1)S(1)}, u32[]{:S(2)}, u32[]{:S(2)}) %all-to-all-start.2) | async-done | bytes 262176 | tf_op jit(solution)/shard_map/all_to_all | solution.py:388
  88.9 0.7 copy-done.2
  89.6 6.6 %warp_adjoint.1 = (f32[128,256]{1,0:T(8,128)}, bf16[128,256]{1,0:T(8,128)(2,1)}) custom-call(s32[7]{0:T(128)} %stack.46.place_ref, s32[2048,1]{1,0:T(8,128)} %reshape_reshape.8.col_ref, s32[1,2048]{1,0:T(1,128)} %reshape_reshape.7.row_ref, bf16[256,64,128]{2,1,0:T(8,128)(2,1)} %bitcast.27, bf16[16,32,256]{2,1,0:T(8,128)(2,1)} %bitcast.31), custom_call_target="tpu_custom_call" | custom-call | bytes 24000000 | tf_op jit(solution)/shard_map/warp_adjoint/pallas_call | solution.py:247
  96.2 3.4 %collective-permute-start.8 = (bf16[128,256]{1,0:T(8,128)(2,1)}, bf16[128,256]{1,0:T(8,128)(2,1)S(1)}, u32[]{:S(2)}, u32[]{:S(2)}) collective-permute-start(bf16[128,256]{1,0:T(8,128)(2,1)} %get-tuple-element.42), channel_id=1, source_target_pairs={{16,0},{32,16},{48,32},{64,48},{80,64},{96,80},{112,96},{128,112},... | collective-permute-start | bytes 196616 | tf_op jit(solution)/shard_map/ppermute | solution.py:390
  99.6 4.5 %collective-permute-done.8 = bf16[128,256]{1,0:T(8,128)(2,1)S(1)} collective-permute-done((bf16[128,256]{1,0:T(8,128)(2,1)}, bf16[128,256]{1,0:T(8,128)(2,1)S(1)}, u32[]{:S(2)}, u32[]{:S(2)}) %collective-permute-start.8) | collective-permute-done | bytes 65568 | tf_op jit(solution)/shard_map/ppermute | solution.py:390
  104.1 1.6 %add_bitcast_fusion = f32[1,16,8,256]{3,2,1,0:T(8,128)} fusion(f32[128,256]{1,0:T(8,128)} %get-tuple-element.41, bf16[128,256]{1,0:T(8,128)(2,1)S(1)} %collective-permute-done.8), kind=kLoop, calls=%fused_computation.1 | loop fusion | flops 65536 | bytes 327680 | tf_op jit(solution)/shard_map/reshape | solution.py:391
  (21 shorter events, 0.1 us)
Async XLA Ops:
  0.0 7.5 %collective-permute-start = (bf16[128,256]{1,0:T(8,128)(2,1)}, bf16[128,256]{1,0:T(8,128)(2,1)S(1)}, u32[]{:S(2)}, u32[]{:S(2)}) collective-permute-start(bf16[128,256]{1,0:T(8,128)(2,1)} %bitcast.37), channel_id=1, source_target_pairs={{0,16},{16,32},{32,48},{48,64},{64,80},{80,96},{96,112},{112,128},... | collective-permute-start | bytes 196616 | tf_op jit(solution)/shard_map/ppermute | solution.py:366
  4.7 26.6 %copy-start.7 = (s32[1,256,2]{1,2,0:T(2,128)S(1)}, s32[1,256,2]{1,2,0:T(2,128)}, u32[]{:S(2)}) copy-start(s32[1,256,2]{1,2,0:T(2,128)} %param.11) | copy-start | bytes 6148
  7.5 25.7 %copy-start.6 = (bf16[128,256]{1,0:T(8,128)(2,1)}, bf16[128,256]{1,0:T(8,128)(2,1)S(1)}, u32[]{:S(2)}) copy-start(bf16[128,256]{1,0:T(8,128)(2,1)S(1)} %collective-permute-done.prior_ref) | copy-start | bytes 196612
  7.5 18.0 %all-to-all-start = ((bf16[16,2,16,256]{3,2,1,0:T(8,128)(2,1)}), bf16[16,2,16,256]{3,2,1,0:T(8,128)(2,1)S(1)}, u32[]{:S(2)}, u32[]{:S(2)}) async-start(bf16[16,2,16,256]{3,2,1,0:T(8,128)(2,1)} %pick_share.1), calls=%async_computation | async-start | bytes 524288 | tf_op jit(solution)/shard_map/all_to_all | solution.py:369
  20.8 19.1 %collective-permute-start.4 = (bf16[2,2,256,256]{3,2,1,0:T(8,128)(2,1)}, bf16[2,2,256,256]{3,2,1,0:T(8,128)(2,1)S(1)}, u32[]{:S(2)}, u32[]{:S(2)}) collective-permute-start(bf16[2,2,256,256]{3,2,1,0:T(8,128)(2,1)} %get-tuple-element.30), channel_id=1, source_target_pairs={{0,1},{1,0},{2,3},{3,2},{4,5},{5,4},{6,7},{7,6},{8,9},{9,8},{10,11... | collective-permute-start | bytes 1572872 | tf_op jit(solution)/shard_map/ppermute | solution.py:372
  22.2 17.7 %collective-permute-start.5 = (bf16[2,2,256,256]{3,2,1,0:T(8,128)(2,1)}, bf16[2,2,256,256]{3,2,1,0:T(8,128)(2,1)S(1)}, u32[]{:S(2)}, u32[]{:S(2)}) collective-permute-start(bf16[2,2,256,256]{3,2,1,0:T(8,128)(2,1)} %get-tuple-element.31), channel_id=1, source_target_pairs={{0,2},{1,3},{2,0},{3,1},{4,6},{5,7},{6,4},{7,5},{8,10},{9,11},{10,... | collective-permute-start | bytes 1572872 | tf_op jit(solution)/shard_map/ppermute | solution.py:372
  25.5 14.4 %collective-permute-start.3 = (bf16[16,2,16,256]{3,2,1,0:T(8,128)(2,1)S(1)}, bf16[16,2,16,256]{3,2,1,0:T(8,128)(2,1)S(1)}, u32[]{:S(2)}, u32[]{:S(2)}) collective-permute-start(bf16[16,2,16,256]{3,2,1,0:T(8,128)(2,1)S(1)} %all-to-all-done), channel_id=1, source_target_pairs={{0,128},{64,192},{128,0},{192,64},{1,129},{65,193},{129,1},{193,65... | collective-permute-start | bytes 786440 | tf_op jit(solution)/shard_map/ppermute | solution.py:382
  28.7 11.3 %collective-permute-start.2 = (bf16[16,2,16,256]{3,2,1,0:T(8,128)(2,1)S(1)}, bf16[16,2,16,256]{3,2,1,0:T(8,128)(2,1)S(1)}, u32[]{:S(2)}, u32[]{:S(2)}) collective-permute-start(bf16[16,2,16,256]{3,2,1,0:T(8,128)(2,1)S(1)} %all-to-all-done), channel_id=1, source_target_pairs={{0,64},{64,128},{128,192},{192,0},{1,65},{65,129},{129,193},{193,1... | collective-permute-start | bytes 786440 | tf_op jit(solution)/shard_map/ppermute | solution.py:382
  29.1 10.9 %collective-permute-start.1 = (bf16[16,2,16,256]{3,2,1,0:T(8,128)(2,1)S(1)}, bf16[16,2,16,256]{3,2,1,0:T(8,128)(2,1)S(1)}, u32[]{:S(2)}, u32[]{:S(2)}) collective-permute-start(bf16[16,2,16,256]{3,2,1,0:T(8,128)(2,1)S(1)} %all-to-all-done), channel_id=1, source_target_pairs={{0,192},{64,0},{128,64},{192,128},{1,193},{65,1},{129,65},{193,129... | collective-permute-start | bytes 786440 | tf_op jit(solution)/shard_map/ppermute | solution.py:382
  39.9 25.6 %copy-start.4 = (bf16[2,2,256,256]{3,2,1,0:T(8,128)(2,1)}, bf16[2,2,256,256]{3,2,1,0:T(8,128)(2,1)S(1)}, u32[]{:S(2)}) copy-start(bf16[2,2,256,256]{3,2,1,0:T(8,128)(2,1)S(1)} %collective-permute-done.4.data1_ref) | copy-start | bytes 1572868
  39.9 0.8 copy-start.5
  40.9 24.6 %copy-start = (bf16[4,16,2,16,256]{4,3,2,1,0:T(8,128)(2,1)}, bf16[4,16,2,16,256]{4,3,2,1,0:T(8,128)(2,1)S(1)}, u32[]{:S(2)}) copy-start(bf16[4,16,2,16,256]{4,3,2,1,0:T(8,128)(2,1)S(1)} %pad_maximum_fusion.own_ref) | copy-start | bytes 3145732
  40.9 24.6 %collective-permute-start.6 = (bf16[4,16,2,16,256]{4,3,2,1,0:T(8,128)(2,1)S(1)}, bf16[4,16,2,16,256]{4,3,2,1,0:T(8,128)(2,1)S(1)}, u32[]{:S(2)}, u32[]{:S(2)}) collective-permute-start(bf16[4,16,2,16,256]{4,3,2,1,0:T(8,128)(2,1)S(1)} %pad_maximum_fusion.own_ref), channel_id=1, source_target_pairs={{0,16},{16,0},{1,17},{17,1},{2,18},{18,2},{3,19},{19,3},{4,20},{20... | collective-permute-start | bytes 3145736 | tf_op jit(solution)/shard_map/ppermute | solution.py:386
  45.2 16.6 %collective-permute-start.7 = (bf16[2,2,256,256]{3,2,1,0:T(8,128)(2,1)}, bf16[2,2,256,256]{3,2,1,0:T(8,128)(2,1)}, u32[]{:S(2)}, u32[]{:S(2)}) collective-permute-start(bf16[2,2,256,256]{3,2,1,0:T(8,128)(2,1)} %get-tuple-element.40), channel_id=1, source_target_pairs={{0,3},{1,2},{2,1},{3,0},{4,7},{5,6},{6,5},{7,4},{8,11},{9,10},{10,... | collective-permute-start | bytes 1572872 | tf_op jit(solution)/shard_map/ppermute | solution.py:372
  45.2 20.3 %all-to-all-start.1 = ((bf16[16,32,256]{2,1,0:T(8,128)(2,1)}), bf16[16,32,256]{2,1,0:T(8,128)(2,1)S(1)}, u32[]{:S(2)}, u32[]{:S(2)}) async-start(bf16[16,32,256]{2,1,0:T(8,128)(2,1)} %warp_forward.1), calls=%async_computation.1 | async-start | bytes 524288 | tf_op jit(solution)/shard_map/all_to_all | solution.py:384
  65.5 0.7 copy-start.1
  65.5 1.1 %copy-start.3 = (bf16[4,16,2,16,256]{4,3,2,1,0:T(8,128)(2,1)}, bf16[4,16,2,16,256]{4,3,2,1,0:T(8,128)(2,1)S(1)}, u32[]{:S(2)}) copy-start(bf16[4,16,2,16,256]{4,3,2,1,0:T(8,128)(2,1)S(1)} %collective-permute-done.6.other_ref) | copy-start | bytes 3145732
  74.7 14.3 %all-to-all-start.2 = ((bf16[16,2,16,256]{3,2,1,0:T(8,128)(2,1)}), bf16[16,2,16,256]{3,2,1,0:T(8,128)(2,1)S(1)}, u32[]{:S(2)}, u32[]{:S(2)}) async-start(bf16[16,2,16,256]{3,2,1,0:T(8,128)(2,1)} %data_gradient.1), calls=%async_computation.2 | async-start | bytes 524288 | tf_op jit(solution)/shard_map/all_to_all | solution.py:388
  88.9 0.7 copy-start.2
  96.2 7.9 %collective-permute-start.8 = (bf16[128,256]{1,0:T(8,128)(2,1)}, bf16[128,256]{1,0:T(8,128)(2,1)S(1)}, u32[]{:S(2)}, u32[]{:S(2)}) collective-permute-start(bf16[128,256]{1,0:T(8,128)(2,1)} %get-tuple-element.42), channel_id=1, source_target_pairs={{16,0},{32,16},{48,32},{64,48},{80,64},{96,80},{112,96},{128,112},... | collective-permute-start | bytes 196616 | tf_op jit(solution)/shard_map/ppermute | solution.py:390

commit v3 on v2

--- a/solution.py
+++ b/solution.py
@@ -11,10 +11,8 @@
 NX = 128
 Z = 8
 SHARE = 4
-PAIR = 4
+PAIR = 8
 STEP = 128
-
-VMEM = 60 * 2**20
 
 F32 = jnp.float32
 BF16 = jnp.bfloat16
@@ -71,8 +69,26 @@
     return as_matrix((to & 15) * Z + ((to >> 4) ^ core) == frm)
 
 
-def warp_kernel(place_ref, col_ref, w_ref, prior_ref, cur_ref, out_ref, acc_ref):
+def fetches(w_ref, slot_ref, sems):
+    return [
+        pltpu.make_async_copy(w_ref.at[pl.ds(i * STEP, STEP)], slot_ref.at[i], sems.at[i]) for i in range(256 // STEP)
+    ]
+
+
+def wait_for(step, copies):
+    for i, copy in enumerate(copies):
+        pl.when(step == i)(copy.wait)
+
+
+def warp_kernel(place_ref, col_ref, w_ref, prior_ref, cur_ref, out_ref, acc_ref, slot_ref, sems):
     step = pl.program_id(0)
+    copies = fetches(w_ref, slot_ref, sems)
+
+    @pl.when(step == 0)
+    def _():
+        for copy in copies:
+            copy.start()
+
     rows = 8 * STEP
     index = col_ref[...]
     r, slot, odd, imag = sublane_roles(rows)
@@ -83,9 +99,10 @@
     v = jnp.where(imag == 1, both[:, 128:], both[:, :128])
     v = jnp.where((index & 1) == odd, v, pltpu.roll(v, 64, 1))
     v = jnp.where(half == odd, v, 0.0)
+    wait_for(step, copies)
     f = lax.dot_general(
         v.reshape(STEP // 4, 32, 128).astype(BF16),
-        w_ref[...].reshape(STEP // 4, 256, 128),
+        slot_ref[step].reshape(STEP // 4, 256, 128),
         (((2,), (2,)), ((0,), (0,))),
         preferred_element_type=F32,
     ).reshape(rows, 256)
@@ -106,12 +123,15 @@
             out_ref[g * SHARE : (g + 1) * SHARE] = turned
 
 
-def adjoint_kernel(place_ref, col_ref, row_ref, w_ref, parts_ref, grad_ref, pulled_ref, image_ref, acc_ref):
+def adjoint_kernel(place_ref, col_ref, row_ref, w_ref, parts_ref, grad_ref, pulled_ref, image_ref, acc_ref, slot_ref, sems):
     step = pl.program_id(0)
+    copies = fetches(w_ref, slot_ref, sems)
     rows = 8 * STEP
 
     @pl.when(step == 0)
     def _():
+        for copy in copies:
+            copy.start()
         total = parts_ref[0:SHARE].astype(F32)
         for g in range(1, 16 // SHARE):
             total = total + parts_ref[g * SHARE : (g + 1) * SHARE].astype(F32)
@@ -137,9 +157,10 @@
     v = shift_lanes(v, slot - odd)
     place4 = (r >> 3) & 3
     v = jnp.concatenate([jnp.where(half == place4, v, 0.0), jnp.where(half + 2 == place4, v, 0.0)], axis=1)
+    wait_for(step, copies)
     f = lax.dot_general(
         v.reshape(STEP // 4, 32, 256).astype(BF16),
-        w_ref[...].reshape(STEP // 4, 256, 128),
+        slot_ref[step].reshape(STEP // 4, 256, 128),
         (((2,), (1,)), ((0,), (0,))),
         preferred_element_type=F32,
     ).reshape(rows, 128)
@@ -159,34 +180,40 @@
 def data_kernel(
     place_ref,
     moved_ref,
-    own_ref,
-    other_ref,
+    own0_ref,
+    own1_ref,
+    own2_ref,
+    own3_ref,
+    other0_ref,
+    other1_ref,
+    other2_ref,
+    other3_ref,
     data0_ref,
     data1_ref,
     data2_ref,
     data3_ref,
     mask_ref,
-    row_ref,
-    back_ref,
-    table_ref,
+    tables_ref,
     out_ref,
     acc_ref,
 ):
+    own_refs = (own0_ref, own1_ref, own2_ref, own3_ref)
+    other_refs = (other0_ref, other1_ref, other2_ref, other3_ref)
     depth, chunk = pl.program_id(0), pl.program_id(1)
     moved = moved_ref[...].reshape(NY, 256).astype(F32)
     image_re, image_im = moved[:, :NX], moved[:, NX:]
     mask = mask_ref[...].astype(F32)
-    table = table_ref[...]
+    row_table, back_table, table = tables_ref[:, :256], tables_ref[:, 256:512], tables_ref[:, 512:]
     sens_re, sens_im, images = [], [], []
     for c in range(PAIR):
-        sens = jnp.where(depth == 0, own_ref[c // 2, :, c % 2], other_ref[c // 2, :, c % 2])
+        sens = jnp.where(depth == 0, own_refs[c // 2][:, c % 2], other_refs[c // 2][:, c % 2])
         sens = sens.reshape(NY, 256).astype(F32)
         sens_re.append(sens[:, :NX])
         sens_im.append(sens[:, NX:])
         re = sens_re[c] * image_re - sens_im[c] * image_im
         im = sens_re[c] * image_im + sens_im[c] * image_re
         images.append(jnp.concatenate([re, im], axis=1).astype(BF16))
-    spectra = matmul(jnp.concatenate(images, axis=0), row_ref[...])
+    spectra = matmul(jnp.concatenate(images, axis=0), row_table)
     tops, bottoms = [], []
     for c in range(PAIR):
         s = spectra[c * NY : (c + 1) * NY]
@@ -207,7 +234,7 @@
     stacked = jnp.concatenate([jnp.concatenate(tops, axis=1), jnp.concatenate(bottoms, axis=1)], axis=0).astype(BF16)
     columns = matmul(table, stacked).astype(BF16)
     rows = jnp.concatenate([columns[:, c * 256 : (c + 1) * 256] for c in range(PAIR)], axis=0)
-    rows = matmul(rows, back_ref[...])
+    rows = matmul(rows, back_table)
     real = imag = 0.0
     for c in range(PAIR):
         b = rows[c * NY : (c + 1) * NY]
@@ -243,17 +270,21 @@
     return pl.BlockSpec(shape, lambda *_: (0,) * len(shape))
 
 
-def call(kernel, place, arrays, grid, in_specs, out_specs, out_shape, scratch, name, micros):
+def call(kernel, place, arrays, grid, in_specs, out_specs, out_shape, scratch, name, micros, vmem):
     return pl.pallas_call(
         kernel,
         grid_spec=pltpu.PrefetchScalarGridSpec(
             num_scalar_prefetch=1, grid=grid, in_specs=in_specs, out_specs=out_specs, scratch_shapes=scratch
         ),
         out_shape=out_shape,
-        compiler_params=pltpu.CompilerParams(vmem_limit_bytes=VMEM),
+        compiler_params=pltpu.CompilerParams(vmem_limit_bytes=vmem * 2**20),
         cost_estimate=pl.CostEstimate(flops=0, bytes_accessed=int(micros * 3e6), transcendentals=0),
         name=name,
     )(place, *arrays)
+
+
+def weight_slots():
+    return pltpu.VMEM((256 // STEP, STEP, 64, 128), BF16), pltpu.SemaphoreType.DMA((256 // STEP,))
 
 
 def warp_forward(place, columns, weights, prior, current):
@@ -265,15 +296,16 @@
         (256 // STEP,),
         [
             pl.BlockSpec((8 * STEP, 1), lambda i, p: (i, 0)),
-            pl.BlockSpec((STEP, 64, 128), lambda i, p: (i, 0, 0)),
+            pl.BlockSpec(memory_space=pltpu.HBM),
             full((128, 256)),
             full((128, 256)),
         ],
         full(shape),
         jax.ShapeDtypeStruct(shape, BF16),
-        [pltpu.VMEM((128, 256), F32)],
+        [pltpu.VMEM((128, 256), F32), *weight_slots()],
         "warp_forward",
         8,
+        32,
     )
 
 
@@ -286,41 +318,38 @@
         [
             pl.BlockSpec((8 * STEP, 1), lambda i, p: (i, 0)),
             pl.BlockSpec((1, 8 * STEP), lambda i, p: (0, i)),
-            pl.BlockSpec((STEP, 64, 128), lambda i, p: (i, 0, 0)),
+            pl.BlockSpec(memory_space=pltpu.HBM),
             full((16, 128 // SHARE, 256)),
         ],
         [full((128, 256)), full((128, 256))],
         [jax.ShapeDtypeStruct((128, 256), F32), jax.ShapeDtypeStruct((128, 256), BF16)],
-        [pltpu.VMEM((128, 256), BF16), pltpu.VMEM((128, 256), F32)],
+        [pltpu.VMEM((128, 256), BF16), pltpu.VMEM((128, 256), F32), *weight_slots()],
         "warp_adjoint",
         8,
+        32,
     )
 
 
 def data_gradient(place, moved, own, other, measured, mask):
     matrix = row_matrix()
-    last = 8 // PAIR - 1
-    sens_block = (PAIR // 2, 16, 2, 16, 256)
     return call(
         data_kernel,
         place,
-        (moved, own, other, *measured, mask, jnp.asarray(matrix), jnp.asarray(matrix.T), jnp.asarray(column_table())),
+        (moved, *own, *other, *measured, mask, jnp.asarray(np.concatenate([matrix, matrix.T, column_table()], axis=1))),
         (2, 8 // PAIR),
         [
             pl.BlockSpec((16, 1, 16, 256), lambda z, c, p: (0, z, 0, 0)),
-            pl.BlockSpec(sens_block, lambda z, c, p: (jnp.where(z == 0, c, last), 0, 0, 0, 0)),
-            pl.BlockSpec(sens_block, lambda z, c, p: (jnp.where(z == 0, 0, c), 0, 0, 0, 0)),
+            *[full((16, 2, 16, 256))] * 8,
             *[pl.BlockSpec((2, 1, NY, 256), lambda z, c, p: (0, z, 0, 0))] * 4,
             full((NY, NX)),
-            full((256, 256)),
-            full((256, 256)),
-            full((NY, 2 * NY)),
+            full((256, 1024)),
         ],
         pl.BlockSpec((16, 1, 16, 256), lambda z, c, p: (0, z, 0, 0)),
         jax.ShapeDtypeStruct((16, 2, 16, 256), BF16),
         [pltpu.VMEM((NY, 256), F32)],
         "data_gradient",
         8,
+        40,
     )
 
 
@@ -336,6 +365,7 @@
         [],
         "pick_share",
         1,
+        60,
     )
 
 
@@ -352,6 +382,7 @@
         [],
         "turn_data",
         3,
+        60,
     )
 
 
@@ -374,16 +405,19 @@
     ]
 
     weights = warp_blocks.reshape(256, 2, 32, 128).transpose(0, 2, 1, 3).reshape(256, 64, 128)
+    weights = pltpu.with_memory_space_constraint(weights, pltpu.HBM)
     index = warp_index[0] - lax.axis_index(coil) * 256
     index = jnp.broadcast_to(index[:, :, None], (256, 2, 4)).reshape(2048)
     columns, rows = index.reshape(2048, 1), index.reshape(1, 2048)
-    prior, sens, measured[0] = lax.optimization_barrier((prior, sens, measured[0]))
+    prior, sens, measured[0], columns = lax.optimization_barrier((prior, sens, measured[0], columns))
     moved = warp_forward(place, columns, weights, prior, current)
-    sens = [sens] + [lax.ppermute(sens, "y", [(i, (i - d) % 4) for i in range(4)]) for d in offsets[1:]]
-    moved, sens, measured[1], measured[2] = lax.optimization_barrier((moved, sens, measured[1], measured[2]))
+    up, down = [(i, (i + 1) % 4) for i in range(4)], [(i, (i - 1) % 4) for i in range(4)]
+    shared = [lax.ppermute(sens, "y", down), lax.ppermute(sens, "y", up)]
+    shared.append(lax.ppermute(shared[0], "y", down))
     moved = lax.all_to_all(moved, coil, 0, 0, tiled=True).reshape(16, 2, 16, 256)
-    sens = jnp.stack(sens)
-    other = lax.ppermute(sens, "core", [(0, 1), (1, 0)])
+    sens = [sens, *shared]
+    other = [lax.ppermute(piece, "core", [(0, 1), (1, 0)]) for piece in sens]
+    moved, sens, other, measured = lax.optimization_barrier((moved, sens, other, measured))
     parts = data_gradient(place, moved, sens, other, measured, sample_mask[0])
     parts = lax.all_to_all(parts, coil, 0, 0, tiled=True).reshape(16, 32, 256)
     grad, pulled = warp_adjoint(place, columns, rows, weights, parts)

time: 106 us -> 92.3 us (0.87)
  waiting for transfers between devices: 31.4 us -> 19.8 us
  Pallas kernels: 29.1 us -> 25.7 us
  starting transfers between devices: 37.3 us -> 40.5 us
  local copies, waits for them, and re-layouts: 6.04 us -> 4.84 us
    ppermute x3, waiting for transfers between devices: 12.3 us -> 0.01 us  [on_device(): lax.ppermute(piece, 'member', [(i, i ^ j) for i in range(SHARE)])]
    pallas_call x5, Pallas kernels: 29.1 us -> 25.7 us  [call(): pl.pallas_call(kernel, grid_spec=pltpu.PrefetchScalarGridSpec(num_scalar_...]
    ppermute x4 -> x7, waiting for transfers between devices: 0.01 us -> 3.02 us  [the longest x2 2.65 us: on_device(): shared = [lax.ppermute(sens, 'y', down), lax.ppermute(sens, 'y', up)]]
    ppermute x1, starting transfers between devices: 3.37 us -> 4.84 us  [on_device(): from_next = lax.ppermute(pulled, loop_axes, backward)]
    ppermute x1, waiting for transfers between devices: 4.48 us -> 3.19 us  [on_device(): from_next = lax.ppermute(pulled, loop_axes, backward)]
    unnamed x16 -> x18, local copies, waits for them, and re-layouts: 2.57 us -> 1.69 us
    ppermute x4 -> x7, starting transfers between devices: 10.1 us -> 10.7 us  [the longest x4 4.68 us: on_device(): other = [lax.ppermute(piece, 'core', [(0, 1), (1, 0)]) for piece in sens]]
  transfers between devices with their start and end apart: 12 -> 15, of which waited for: 5 -> 6; matrix products, arithmetic and copies ran while one was open for 3% -> 3% of each run, Pallas kernels for 14% -> 15%
where the time goes in v3:
time: 92.3 us; the launch traced here: 91.8 us
  starting transfers between devices  40.5 us (44%)
  Pallas kernels  25.7 us (28%)
  waiting for transfers between devices  19.8 us (21%)
  local copies, waits for them, and re-layouts  4.84 us (5%)
    pallas_call x5, Pallas kernels, call(): pl.pallas_call(kernel, grid_spec=pltpu.PrefetchScalarGridSpec(num_scalar_...  25.7 us
    all_to_all x1, waiting for transfers between devices, on_device(): parts = lax.all_to_all(parts, coil, 0, 0, tiled=True).reshape(16, 32, 256)  8.42 us
    all_to_all x1, starting transfers between devices, on_device(): sens = lax.all_to_all(sens, coil, 0, 0, tiled=True)  8.32 us
    ppermute x1, starting transfers between devices, on_device(): from_next = lax.ppermute(pulled, loop_axes, backward)  4.84 us
    all_to_all x1, starting transfers between devices, on_device(): lax.all_to_all(moved, coil, 0, 0, tiled=True).reshape(16, 2, 16, 256)  4.73 us
    ppermute x4, starting transfers between devices, on_device(): other = [lax.ppermute(piece, 'core', [(0, 1), (1, 0)]) for piece in sens]  4.68 us
    all_to_all x1, starting transfers between devices, on_device(): parts = lax.all_to_all(parts, coil, 0, 0, tiled=True).reshape(16, 32, 256)  4.55 us
    ppermute x1, starting transfers between devices, on_device(): prior = lax.ppermute(current, loop_axes, forward)  4.13 us
  transfers between devices with their start and end apart: 15, of which 6 were waited for; matrix products, arithmetic and copies ran while one was open for 3% of the time, Pallas kernels for 15%

profile of v3, /device:TPU:1, one launch (start us, length us, event | category | flops | bytes accessed | tf_op | source)
XLA Modules:
  0.0 91.8 jit_solution(5459711701535814395)
XLA Ops:
  0.0 4.1 %collective-permute-start = (bf16[128,256]{1,0:T(8,128)(2,1)}, bf16[128,256]{1,0:T(8,128)(2,1)S(1)}, u32[]{:S(2)}, u32[]{:S(2)}) collective-permute-start(bf16[128,256]{1,0:T(8,128)(2,1)} %bitcast.25), channel_id=1, source_target_pairs={{0,16},{16,32},{32,48},{48,64},{64,80},{80,96},{96,112},{112,128},... | collective-permute-start | bytes 196616 | tf_op jit(solution)/shard_map/ppermute | solution.py:397
  4.1 0.7 stack.31.place_ref
  4.8 2.6 %pick_share.1 = bf16[16,2,16,256]{3,2,1,0:T(8,128)(2,1)} custom-call(s32[7]{0:T(128)} %stack.31.place_ref, bf16[4,4,2,128,256]{4,3,2,1,0:T(8,128)(2,1)} %bitcast.29), custom_call_target="tpu_custom_call" | custom-call | bytes 3000000 | tf_op jit(solution)/shard_map/pick_share/pallas_call | solution.py:274
  7.5 8.3 %all-to-all-start = ((bf16[16,2,16,256]{3,2,1,0:T(8,128)(2,1)}), bf16[16,2,16,256]{3,2,1,0:T(8,128)(2,1)S(1)}, u32[]{:S(2)}, u32[]{:S(2)}) async-start(bf16[16,2,16,256]{3,2,1,0:T(8,128)(2,1)} %pick_share.1), calls=%async_computation | async-start | bytes 524288 | tf_op jit(solution)/shard_map/all_to_all | solution.py:400
  16.0 0.3 broadcast_in_dim.2
  16.3 0.3 reshape_reshape.6
  16.7 5.0 %turn_data.1 = (bf16[2,2,256,256]{3,2,1,0:T(8,128)(2,1)}, bf16[2,2,256,256]{3,2,1,0:T(8,128)(2,1)}, bf16[2,2,256,256]{3,2,1,0:T(8,128)(2,1)}, bf16[2,2,256,256]{3,2,1,0:T(8,128)(2,1)}) custom-call(s32[7]{0:T(128)} %stack.31.place_ref, bf16[2,16,128,256]{3,2,1,0:T(8,128)(2,1)} %bitcast.30), custom_call_target="tpu_custom_call" | custom-call | bytes 9000000 | tf_op jit(solution)/shard_map/turn_data/pallas_call | solution.py:274
  21.7 1.4 %collective-permute-start.8 = (bf16[2,2,256,256]{3,2,1,0:T(8,128)(2,1)}, bf16[2,2,256,256]{3,2,1,0:T(8,128)(2,1)S(1)}, u32[]{:S(2)}, u32[]{:S(2)}) collective-permute-start(bf16[2,2,256,256]{3,2,1,0:T(8,128)(2,1)} %get-tuple-element.39), channel_id=1, source_target_pairs={{0,1},{1,0},{2,3},{3,2},{4,5},{5,4},{6,7},{7,6},{8,9},{9,8},{10,11... | collective-permute-start | bytes 1572872 | tf_op jit(solution)/shard_map/ppermute | solution.py:403
  23.0 1.2 %collective-permute-start.9 = (bf16[2,2,256,256]{3,2,1,0:T(8,128)(2,1)}, bf16[2,2,256,256]{3,2,1,0:T(8,128)(2,1)}, u32[]{:S(2)}, u32[]{:S(2)}) collective-permute-start(bf16[2,2,256,256]{3,2,1,0:T(8,128)(2,1)} %get-tuple-element.40), channel_id=1, source_target_pairs={{0,2},{1,3},{2,0},{3,1},{4,6},{5,7},{6,4},{7,5},{8,10},{9,11},{10,... | collective-permute-start | bytes 1572872 | tf_op jit(solution)/shard_map/ppermute | solution.py:403
  24.2 1.2 %all-to-all-done.own0_ref = bf16[16,2,16,256]{3,2,1,0:T(8,128)(2,1)S(1)} async-done(((bf16[16,2,16,256]{3,2,1,0:T(8,128)(2,1)}), bf16[16,2,16,256]{3,2,1,0:T(8,128)(2,1)S(1)}, u32[]{:S(2)}, u32[]{:S(2)}) %all-to-all-start) | async-done | bytes 262176 | tf_op jit(solution)/shard_map/all_to_all | solution.py:400
  25.4 2.9 %collective-permute-start.1 = (bf16[16,2,16,256]{3,2,1,0:T(8,128)(2,1)S(1)}, bf16[16,2,16,256]{3,2,1,0:T(8,128)(2,1)S(1)}, u32[]{:S(2)}, u32[]{:S(2)}) collective-permute-start(bf16[16,2,16,256]{3,2,1,0:T(8,128)(2,1)S(1)} %all-to-all-done.own0_ref), channel_id=1, source_target_pairs={{0,192},{64,0},{128,64},{192,128},{1,193},{65,1},{129,65},{193,129... | collective-permute-start | bytes 786440 | tf_op jit(solution)/shard_map/ppermute | solution.py:415
  28.3 0.7 collective-permute-start.10
  29.0 2.6 %collective-permute-done.1.own1_ref = bf16[16,2,16,256]{3,2,1,0:T(8,128)(2,1)S(1)} collective-permute-done((bf16[16,2,16,256]{3,2,1,0:T(8,128)(2,1)S(1)}, bf16[16,2,16,256]{3,2,1,0:T(8,128)(2,1)S(1)}, u32[]{:S(2)}, u32[]{:S(2)}) %collective-permute-start.1) | collective-permute-done | bytes 262176 | tf_op jit(solution)/shard_map/ppermute | solution.py:415
  31.7 3.1 %collective-permute-start.3 = (bf16[16,2,16,256]{3,2,1,0:T(8,128)(2,1)S(1)}, bf16[16,2,16,256]{3,2,1,0:T(8,128)(2,1)}, u32[]{:S(2)}, u32[]{:S(2)}) collective-permute-start(bf16[16,2,16,256]{3,2,1,0:T(8,128)(2,1)S(1)} %collective-permute-done.1.own1_ref), channel_id=1, source_target_pairs={{0,192},{64,0},{128,64},{192,128},{1,193},{65,1},{129,65},{193,129... | collective-permute-start | bytes 786440 | tf_op jit(solution)/shard_map/ppermute | solution.py:416
  34.8 0.4 copy.13.col_ref
  35.2 6.4 %warp_forward.1 = bf16[16,32,256]{2,1,0:T(8,128)(2,1)} custom-call(s32[7]{0:T(128)S(1)} %copy-done.6, s32[2048,1]{1,0:T(8,128)S(1)} %copy.13.col_ref, bf16[256,64,128]{2,1,0:T(8,128)(2,1)} %bitcast.27, bf16[128,256]{1,0:T(8,128)(2,1)S(1)} %collective-permute-done.prior_ref, bf16[128,256]{1,0:T(8,128)(2,1)S(1)} %bitcast.26), custom_call_target="tpu_custom_call" | custom-call | bytes 24000000 | tf_op jit(solution)/shard_map/warp_forward/pallas_call | solution.py:274
  41.6 4.7 %all-to-all-start.1 = ((bf16[16,32,256]{2,1,0:T(8,128)(2,1)}), bf16[16,32,256]{2,1,0:T(8,128)(2,1)S(1)}, u32[]{:S(2)}, u32[]{:S(2)}) async-start(bf16[16,32,256]{2,1,0:T(8,128)(2,1)} %warp_forward.1), calls=%async_computation.1 | async-start | bytes 524288 | tf_op jit(solution)/shard_map/all_to_all | solution.py:417
  46.3 3.9 %collective-permute-start.4 = (bf16[16,2,16,256]{3,2,1,0:T(8,128)(2,1)S(1)}, bf16[16,2,16,256]{3,2,1,0:T(8,128)(2,1)S(1)}, u32[]{:S(2)}, u32[]{:S(2)}) collective-permute-start(bf16[16,2,16,256]{3,2,1,0:T(8,128)(2,1)S(1)} %all-to-all-done.own0_ref), channel_id=1, source_target_pairs={{0,16},{16,0},{1,17},{17,1},{2,18},{18,2},{3,19},{19,3},{4,20},{20... | collective-permute-start | bytes 786440 | tf_op jit(solution)/shard_map/ppermute | solution.py:419
  50.4 0.4 collective-permute-start.6
  50.8 0.3 collective-permute-start.7
  51.0 0.4 collective-permute-done.4.other0_ref
  51.4 0.7 copy-done.2
  52.1 3.9 %all-to-all-done.1 = bf16[16,32,256]{2,1,0:T(8,128)(2,1)S(1)} async-done(((bf16[16,32,256]{2,1,0:T(8,128)(2,1)}), bf16[16,32,256]{2,1,0:T(8,128)(2,1)S(1)}, u32[]{:S(2)}, u32[]{:S(2)}) %all-to-all-start.1) | async-done | bytes 262176 | tf_op jit(solution)/shard_map/all_to_all | solution.py:417
  56.1 0.9 %copy-done.3 = bf16[16,2,16,256]{3,2,1,0:T(8,128)(2,1)S(1)} copy-done((bf16[16,2,16,256]{3,2,1,0:T(8,128)(2,1)S(1)}, bf16[16,2,16,256]{3,2,1,0:T(8,128)(2,1)}, u32[]{:S(2)}) %copy-start.3) | copy-done | bytes 262168
  57.0 6.9 %data_gradient.1 = bf16[16,2,16,256]{3,2,1,0:T(8,128)(2,1)} custom-call(s32[7]{0:T(128)S(1)} %copy-done.6, bf16[16,2,16,256]{3,2,1,0:T(8,128)(2,1)S(1)} %bitcast.22, bf16[16,2,16,256]{3,2,1,0:T(8,128)(2,1)S(1)} %all-to-all-done.own0_ref, bf16[16,2,16,256]{3,2,1,0:T(8,128)(2,1)S(1)} %collective-permute-done.1.own1_ref, ...), custom_call_target="tpu_custom_call" | custom-call | bytes 24000000 | tf_op jit(solution)/shard_map/data_gradient/pallas_call | solution.py:274
  63.9 4.6 %all-to-all-start.2 = ((bf16[16,2,16,256]{3,2,1,0:T(8,128)(2,1)}), bf16[16,2,16,256]{3,2,1,0:T(8,128)(2,1)S(1)}, u32[]{:S(2)}, u32[]{:S(2)}) async-start(bf16[16,2,16,256]{3,2,1,0:T(8,128)(2,1)} %data_gradient.1), calls=%async_computation.2 | async-start | bytes 524288 | tf_op jit(solution)/shard_map/all_to_all | solution.py:422
  68.5 1.3 %reshape_reshape.7.row_ref = s32[1,2048]{1,0:T(1,128)S(1)} reshape(s32[256,2,4]{2,1,0:T(2,128)} %copy-done.7) | data formatting | bytes 16384 | tf_op jit(solution)/shard_map/reshape;reshape | solution.py:411
  69.8 8.4 %all-to-all-done.2 = bf16[16,2,16,256]{3,2,1,0:T(8,128)(2,1)S(1)} async-done(((bf16[16,2,16,256]{3,2,1,0:T(8,128)(2,1)}), bf16[16,2,16,256]{3,2,1,0:T(8,128)(2,1)S(1)}, u32[]{:S(2)}, u32[]{:S(2)}) %all-to-all-start.2) | async-done | bytes 262176 | tf_op jit(solution)/shard_map/all_to_all | solution.py:422
  78.2 4.8 %warp_adjoint.1 = (f32[128,256]{1,0:T(8,128)S(1)}, bf16[128,256]{1,0:T(8,128)(2,1)S(1)}) custom-call(s32[7]{0:T(128)S(1)} %copy-done.6, s32[2048,1]{1,0:T(8,128)S(1)} %copy.13.col_ref, s32[1,2048]{1,0:T(1,128)S(1)} %reshape_reshape.7.row_ref, bf16[256,64,128]{2,1,0:T(8,128)(2,1)} %bitcast.28, bf16[16,32,256]{2,1,0:T(8,128)(2,1)S(1)} %bitcast.23), custom_call_target="tpu_custom_call" | custom-call | bytes 24000000 | tf_op jit(solution)/shard_map/warp_adjoint/pallas_call | solution.py:274
  83.1 4.8 %collective-permute-start.11 = (bf16[128,256]{1,0:T(8,128)(2,1)S(1)}, bf16[128,256]{1,0:T(8,128)(2,1)S(1)}, u32[]{:S(2)}, u32[]{:S(2)}) collective-permute-start(bf16[128,256]{1,0:T(8,128)(2,1)S(1)} %get-tuple-element.56), channel_id=1, source_target_pairs={{16,0},{32,16},{48,32},{64,48},{80,64},{96,80},{112,96},{128,112},... | collective-permute-start | bytes 196616 | tf_op jit(solution)/shard_map/ppermute | solution.py:424
  87.9 3.2 %collective-permute-done.11 = bf16[128,256]{1,0:T(8,128)(2,1)S(1)} collective-permute-done((bf16[128,256]{1,0:T(8,128)(2,1)S(1)}, bf16[128,256]{1,0:T(8,128)(2,1)S(1)}, u32[]{:S(2)}, u32[]{:S(2)}) %collective-permute-start.11) | collective-permute-done | bytes 65568 | tf_op jit(solution)/shard_map/ppermute | solution.py:424
  91.1 0.7 add_bitcast_fusion
  (29 shorter events, 0.3 us)
Async XLA Ops:
  0.0 15.8 %copy-start.8 = (s32[1,256,2]{1,2,0:T(2,128)S(1)}, s32[1,256,2]{1,2,0:T(2,128)}, u32[]{:S(2)}) copy-start(s32[1,256,2]{1,2,0:T(2,128)} %param.9) | copy-start | bytes 6148
  0.0 7.5 %collective-permute-start = (bf16[128,256]{1,0:T(8,128)(2,1)}, bf16[128,256]{1,0:T(8,128)(2,1)S(1)}, u32[]{:S(2)}, u32[]{:S(2)}) collective-permute-start(bf16[128,256]{1,0:T(8,128)(2,1)} %bitcast.25), channel_id=1, source_target_pairs={{0,16},{16,32},{32,48},{48,64},{64,80},{80,96},{96,112},{112,128},... | collective-permute-start | bytes 196616 | tf_op jit(solution)/shard_map/ppermute | solution.py:397
  7.5 18.0 %all-to-all-start = ((bf16[16,2,16,256]{3,2,1,0:T(8,128)(2,1)}), bf16[16,2,16,256]{3,2,1,0:T(8,128)(2,1)S(1)}, u32[]{:S(2)}, u32[]{:S(2)}) async-start(bf16[16,2,16,256]{3,2,1,0:T(8,128)(2,1)} %pick_share.1), calls=%async_computation | async-start | bytes 524288 | tf_op jit(solution)/shard_map/all_to_all | solution.py:400
  15.8 19.4 %copy-start.5 = (bf16[1,16,8,256]{3,2,1,0:T(8,128)(2,1)S(1)}, bf16[1,16,8,256]{3,2,1,0:T(8,128)(2,1)}, u32[]{:S(2)}) copy-start(bf16[1,16,8,256]{3,2,1,0:T(8,128)(2,1)} %param.7) | copy-start | bytes 196612
  15.8 19.4 %copy-start.6 = (s32[7]{0:T(128)S(1)}, s32[7]{0:T(128)}, u32[]{:S(2)}) copy-start(s32[7]{0:T(128)} %stack.31.place_ref) | copy-start | bytes 88
  16.3 15.3 %copy-start.7 = (s32[256,2,4]{2,1,0:T(2,128)}, s32[256,2,4]{2,1,0:T(2,128)S(1)}, u32[]{:S(2)}) copy-start(s32[256,2,4]{2,1,0:T(2,128)S(1)} %broadcast_in_dim.2) | copy-start | bytes 24580
  21.7 24.7 %collective-permute-start.8 = (bf16[2,2,256,256]{3,2,1,0:T(8,128)(2,1)}, bf16[2,2,256,256]{3,2,1,0:T(8,128)(2,1)S(1)}, u32[]{:S(2)}, u32[]{:S(2)}) collective-permute-start(bf16[2,2,256,256]{3,2,1,0:T(8,128)(2,1)} %get-tuple-element.39), channel_id=1, source_target_pairs={{0,1},{1,0},{2,3},{3,2},{4,5},{5,4},{6,7},{7,6},{8,9},{9,8},{10,11... | collective-permute-start | bytes 1572872 | tf_op jit(solution)/shard_map/ppermute | solution.py:403
  23.0 27.2 %collective-permute-start.9 = (bf16[2,2,256,256]{3,2,1,0:T(8,128)(2,1)}, bf16[2,2,256,256]{3,2,1,0:T(8,128)(2,1)}, u32[]{:S(2)}, u32[]{:S(2)}) collective-permute-start(bf16[2,2,256,256]{3,2,1,0:T(8,128)(2,1)} %get-tuple-element.40), channel_id=1, source_target_pairs={{0,2},{1,3},{2,0},{3,1},{4,6},{5,7},{6,4},{7,5},{8,10},{9,11},{10,... | collective-permute-start | bytes 1572872 | tf_op jit(solution)/shard_map/ppermute | solution.py:403
  25.4 6.2 %collective-permute-start.1 = (bf16[16,2,16,256]{3,2,1,0:T(8,128)(2,1)S(1)}, bf16[16,2,16,256]{3,2,1,0:T(8,128)(2,1)S(1)}, u32[]{:S(2)}, u32[]{:S(2)}) collective-permute-start(bf16[16,2,16,256]{3,2,1,0:T(8,128)(2,1)S(1)} %all-to-all-done.own0_ref), channel_id=1, source_target_pairs={{0,192},{64,0},{128,64},{192,128},{1,193},{65,1},{129,65},{193,129... | collective-permute-start | bytes 786440 | tf_op jit(solution)/shard_map/ppermute | solution.py:415
  28.3 22.7 %collective-permute-start.10 = (bf16[2,2,256,256]{3,2,1,0:T(8,128)(2,1)}, bf16[2,2,256,256]{3,2,1,0:T(8,128)(2,1)}, u32[]{:S(2)}, u32[]{:S(2)}) collective-permute-start(bf16[2,2,256,256]{3,2,1,0:T(8,128)(2,1)} %get-tuple-element.41), channel_id=1, source_target_pairs={{0,3},{1,2},{2,1},{3,0},{4,7},{5,6},{6,5},{7,4},{8,11},{9,10},{10,... | collective-permute-start | bytes 1572872 | tf_op jit(solution)/shard_map/ppermute | solution.py:403
  29.0 21.3 %collective-permute-start.2 = (bf16[16,2,16,256]{3,2,1,0:T(8,128)(2,1)S(1)}, bf16[16,2,16,256]{3,2,1,0:T(8,128)(2,1)}, u32[]{:S(2)}, u32[]{:S(2)}) collective-permute-start(bf16[16,2,16,256]{3,2,1,0:T(8,128)(2,1)S(1)} %all-to-all-done.own0_ref), channel_id=1, source_target_pairs={{0,64},{64,128},{128,192},{192,0},{1,65},{65,129},{129,193},{193,1... | collective-permute-start | bytes 786440 | tf_op jit(solution)/shard_map/ppermute | solution.py:415
  31.7 19.1 %collective-permute-start.3 = (bf16[16,2,16,256]{3,2,1,0:T(8,128)(2,1)S(1)}, bf16[16,2,16,256]{3,2,1,0:T(8,128)(2,1)}, u32[]{:S(2)}, u32[]{:S(2)}) collective-permute-start(bf16[16,2,16,256]{3,2,1,0:T(8,128)(2,1)S(1)} %collective-permute-done.1.own1_ref), channel_id=1, source_target_pairs={{0,192},{64,0},{128,64},{192,128},{1,193},{65,1},{129,65},{193,129... | collective-permute-start | bytes 786440 | tf_op jit(solution)/shard_map/ppermute | solution.py:416
  35.2 20.9 %copy-start = (bf16[256,1024]{1,0:T(8,128)(2,1)S(1)}, bf16[256,1024]{1,0:T(8,128)(2,1)}, u32[]{:S(2)}) copy-start(bf16[256,1024]{1,0:T(8,128)(2,1)} %constant.52.clone.tables_ref) | copy-start | bytes 1572868
  35.2 20.9 %copy-start.1 = (bf16[2,2,256,256]{3,2,1,0:T(8,128)(2,1)S(1)}, bf16[2,2,256,256]{3,2,1,0:T(8,128)(2,1)}, u32[]{:S(2)}) copy-start(bf16[2,2,256,256]{3,2,1,0:T(8,128)(2,1)} %get-tuple-element.51.data0_ref) | copy-start | bytes 1572868
  35.2 20.9 %copy-start.4 = (s32[1,256,128]{2,1,0:T(8,128)S(1)}, s32[1,256,128]{2,1,0:T(8,128)}, u32[]{:S(2)}) copy-start(s32[1,256,128]{2,1,0:T(8,128)} %param.10) | copy-start | bytes 393220
  41.6 14.5 %all-to-all-start.1 = ((bf16[16,32,256]{2,1,0:T(8,128)(2,1)}), bf16[16,32,256]{2,1,0:T(8,128)(2,1)S(1)}, u32[]{:S(2)}, u32[]{:S(2)}) async-start(bf16[16,32,256]{2,1,0:T(8,128)(2,1)} %warp_forward.1), calls=%async_computation.1 | async-start | bytes 524288 | tf_op jit(solution)/shard_map/all_to_all | solution.py:417
  46.3 5.1 %collective-permute-start.4 = (bf16[16,2,16,256]{3,2,1,0:T(8,128)(2,1)S(1)}, bf16[16,2,16,256]{3,2,1,0:T(8,128)(2,1)S(1)}, u32[]{:S(2)}, u32[]{:S(2)}) collective-permute-start(bf16[16,2,16,256]{3,2,1,0:T(8,128)(2,1)S(1)} %all-to-all-done.own0_ref), channel_id=1, source_target_pairs={{0,16},{16,0},{1,17},{17,1},{2,18},{18,2},{3,19},{19,3},{4,20},{20... | collective-permute-start | bytes 786440 | tf_op jit(solution)/shard_map/ppermute | solution.py:419
  50.2 5.8 %collective-permute-start.5 = (bf16[16,2,16,256]{3,2,1,0:T(8,128)(2,1)S(1)}, bf16[16,2,16,256]{3,2,1,0:T(8,128)(2,1)}, u32[]{:S(2)}, u32[]{:S(2)}) collective-permute-start(bf16[16,2,16,256]{3,2,1,0:T(8,128)(2,1)S(1)} %collective-permute-done.1.own1_ref), channel_id=1, source_target_pairs={{0,16},{16,0},{1,17},{17,1},{2,18},{18,2},{3,19},{19,3},{4,20},{20... | collective-permute-start | bytes 786440 | tf_op jit(solution)/shard_map/ppermute | solution.py:419
  50.4 5.7 %collective-permute-start.6 = (bf16[16,2,16,256]{3,2,1,0:T(8,128)(2,1)}, bf16[16,2,16,256]{3,2,1,0:T(8,128)(2,1)}, u32[]{:S(2)}, u32[]{:S(2)}) collective-permute-start(bf16[16,2,16,256]{3,2,1,0:T(8,128)(2,1)} %collective-permute-done.2.own2_ref), channel_id=1, source_target_pairs={{0,16},{16,0},{1,17},{17,1},{2,18},{18,2},{3,19},{19,3},{4,20},{20... | collective-permute-start | bytes 786440 | tf_op jit(solution)/shard_map/ppermute | solution.py:419
  50.8 5.3 %collective-permute-start.7 = (bf16[16,2,16,256]{3,2,1,0:T(8,128)(2,1)}, bf16[16,2,16,256]{3,2,1,0:T(8,128)(2,1)}, u32[]{:S(2)}, u32[]{:S(2)}) collective-permute-start(bf16[16,2,16,256]{3,2,1,0:T(8,128)(2,1)} %collective-permute-done.3.own3_ref), channel_id=1, source_target_pairs={{0,16},{16,0},{1,17},{17,1},{2,18},{18,2},{3,19},{19,3},{4,20},{20... | collective-permute-start | bytes 786440 | tf_op jit(solution)/shard_map/ppermute | solution.py:419
  51.4 0.7 copy-start.2
  56.1 1.0 %copy-start.3 = (bf16[16,2,16,256]{3,2,1,0:T(8,128)(2,1)S(1)}, bf16[16,2,16,256]{3,2,1,0:T(8,128)(2,1)}, u32[]{:S(2)}) copy-start(bf16[16,2,16,256]{3,2,1,0:T(8,128)(2,1)} %copy-done.2) | copy-start | bytes 786436
  63.9 14.3 %all-to-all-start.2 = ((bf16[16,2,16,256]{3,2,1,0:T(8,128)(2,1)}), bf16[16,2,16,256]{3,2,1,0:T(8,128)(2,1)S(1)}, u32[]{:S(2)}, u32[]{:S(2)}) async-start(bf16[16,2,16,256]{3,2,1,0:T(8,128)(2,1)} %data_gradient.1), calls=%async_computation.2 | async-start | bytes 524288 | tf_op jit(solution)/shard_map/all_to_all | solution.py:422
  83.1 8.0 %collective-permute-start.11 = (bf16[128,256]{1,0:T(8,128)(2,1)S(1)}, bf16[128,256]{1,0:T(8,128)(2,1)S(1)}, u32[]{:S(2)}, u32[]{:S(2)}) collective-permute-start(bf16[128,256]{1,0:T(8,128)(2,1)S(1)} %get-tuple-element.56), channel_id=1, source_target_pairs={{16,0},{32,16},{48,32},{64,48},{80,64},{96,80},{112,96},{128,112},... | collective-permute-start | bytes 196616 | tf_op jit(solution)/shard_map/ppermute | solution.py:424

commit v4 on v3

--- a/solution.py
+++ b/solution.py
@@ -249,7 +249,7 @@
 
 def pick_kernel(place_ref, sens_ref, out_ref):
     to, frm = iota((64, 128), 0), iota((64, 128), 1)
-    turn = as_matrix((to & 15) * Z + (to >> 4) * 2 + place_ref[1] == frm)
+    turn = as_matrix((to & 15) * Z + (to >> 4) * 2 + (place_ref[0] & 1) == frm)
     for g in range(16 // SHARE):
         for c in range(2):
             picked = matmul(turn, sens_ref[g, 0, c]).astype(BF16)
@@ -359,7 +359,7 @@
         place,
         (sensitivity.reshape(4, 4, 2, 128, 256),),
         (1,),
-        [pl.BlockSpec((4, 1, 2, 128, 256), lambda g, p: (0, p[0], 0, 0, 0))],
+        [pl.BlockSpec((4, 1, 2, 128, 256), lambda g, p: (0, p[0] >> 1, 0, 0, 0))],
         full((16, 2, 16, 256)),
         jax.ShapeDtypeStruct((16, 2, 16, 256), BF16),
         [],
@@ -370,7 +370,7 @@
 
 
 def turn_data(place, data):
-    blocks = 8
+    blocks = 16
     return call(
         turn_kernel,
         place,
@@ -396,7 +396,7 @@
     current = cine_image.reshape(128, 256)
     prior = lax.ppermute(current, loop_axes, forward)
 
-    sens, prior, kspace_data = lax.optimization_barrier((pick_share(place, sensitivity), prior, kspace_data))
+    sens, prior, kspace_data = lax.optimization_barrier((pick_share((row * 2 + core).reshape(1), sensitivity), prior, kspace_data))
     sens = lax.all_to_all(sens, coil, 0, 0, tiled=True)
     measured = turn_data(place, kspace_data)
     measured = [
@@ -418,6 +418,7 @@
     sens = [sens, *shared]
     other = [lax.ppermute(piece, "core", [(0, 1), (1, 0)]) for piece in sens]
     moved, sens, other, measured = lax.optimization_barrier((moved, sens, other, measured))
+    other = [pltpu.with_memory_space_constraint(piece, pltpu.HBM) for piece in other]
     parts = data_gradient(place, moved, sens, other, measured, sample_mask[0])
     parts = lax.all_to_all(parts, coil, 0, 0, tiled=True).reshape(16, 32, 256)
     grad, pulled = warp_adjoint(place, columns, rows, weights, parts)

time: 92.3 us -> 91.7 us (level)
  starting transfers between devices: 40.5 us -> 43.2 us
  Pallas kernels: 25.7 us -> 24 us
  local copies, waits for them, and re-layouts: 4.84 us -> 3.18 us
    ppermute x4, starting transfers between devices: 4.68 us -> 6.89 us  [on_device(): other = [lax.ppermute(piece, 'core', [(0, 1), (1, 0)]) for piece in sens]]
    all_to_all x1, starting transfers between devices: 4.55 us -> 6.61 us  [on_device(): parts = lax.all_to_all(parts, coil, 0, 0, tiled=True).reshape(16, 32, 256)]
    pallas_call x5, Pallas kernels: 25.7 us -> 24 us  [call(): pl.pallas_call(kernel, grid_spec=pltpu.PrefetchScalarGridSpec(num_scalar_...]
    unnamed x18 -> x14, local copies, waits for them, and re-layouts: 1.69 us -> 0.04 us
    all_to_all x1, waiting for transfers between devices: 3.94 us -> 2.46 us  [on_device(): lax.all_to_all(moved, coil, 0, 0, tiled=True).reshape(16, 2, 16, 256)]
  transfers between devices with their start and end apart: 15 -> 15, of which waited for: 6 -> 6; matrix products, arithmetic and copies ran while one was open for 3% -> 3% of each run, Pallas kernels for 15% -> 13%
where the time goes in v4:
time: 91.7 us; the launch traced here: 91.2 us
  starting transfers between devices  43.2 us (47%)
  Pallas kernels  24 us (26%)
  waiting for transfers between devices  19.9 us (22%)
  local copies, waits for them, and re-layouts  3.18 us (3%)
    pallas_call x5, Pallas kernels, call(): pl.pallas_call(kernel, grid_spec=pltpu.PrefetchScalarGridSpec(num_scalar_...  24 us
    all_to_all x1, waiting for transfers between devices, on_device(): parts = lax.all_to_all(parts, coil, 0, 0, tiled=True).reshape(16, 32, 256)  8.42 us
    all_to_all x1, starting transfers between devices, on_device(): sens = lax.all_to_all(sens, coil, 0, 0, tiled=True)  8.32 us
    ppermute x4, starting transfers between devices, on_device(): other = [lax.ppermute(piece, 'core', [(0, 1), (1, 0)]) for piece in sens]  6.89 us
    all_to_all x1, starting transfers between devices, on_device(): parts = lax.all_to_all(parts, coil, 0, 0, tiled=True).reshape(16, 32, 256)  6.61 us
    ppermute x1, starting transfers between devices, on_device(): from_next = lax.ppermute(pulled, loop_axes, backward)  4.85 us
    ppermute x1, starting transfers between devices, on_device(): prior = lax.ppermute(current, loop_axes, forward)  4.13 us
    all_to_all x1, starting transfers between devices, on_device(): lax.all_to_all(moved, coil, 0, 0, tiled=True).reshape(16, 2, 16, 256)  3.94 us
  transfers between devices with their start and end apart: 15, of which 6 were waited for; matrix products, arithmetic and copies ran while one was open for 3% of the time, Pallas kernels for 13%

profile of v4, /device:TPU:1, one launch (start us, length us, event | category | flops | bytes accessed | tf_op | source)
XLA Modules:
  0.0 91.2 jit_solution(14974271806604879769)
XLA Ops:
  0.0 4.1 %collective-permute-start = (bf16[128,256]{1,0:T(8,128)(2,1)}, bf16[128,256]{1,0:T(8,128)(2,1)S(1)}, u32[]{:S(2)}, u32[]{:S(2)}) collective-permute-start(bf16[128,256]{1,0:T(8,128)(2,1)} %bitcast.26), channel_id=1, source_target_pairs={{0,16},{16,32},{32,48},{48,64},{64,80},{80,96},{96,112},{112,128},... | collective-permute-start | bytes 196616 | tf_op jit(solution)/shard_map/ppermute | solution.py:397
  4.1 2.0 %pick_share.1 = bf16[16,2,16,256]{3,2,1,0:T(8,128)(2,1)} custom-call(s32[1]{0:T(128)} %bitcast.7.place_ref, bf16[4,4,2,128,256]{4,3,2,1,0:T(8,128)(2,1)} %bitcast.30), custom_call_target="tpu_custom_call" | custom-call | bytes 3000000 | tf_op jit(solution)/shard_map/pick_share/pallas_call | solution.py:274
  6.1 8.3 %all-to-all-start = ((bf16[16,2,16,256]{3,2,1,0:T(8,128)(2,1)}), bf16[16,2,16,256]{3,2,1,0:T(8,128)(2,1)S(1)}, u32[]{:S(2)}, u32[]{:S(2)}) async-start(bf16[16,2,16,256]{3,2,1,0:T(8,128)(2,1)} %pick_share.1), calls=%async_computation | async-start | bytes 524288 | tf_op jit(solution)/shard_map/all_to_all | solution.py:400
  14.5 0.1 copy.10
  14.7 0.3 broadcast_in_dim.2
  15.0 0.3 reshape_reshape.6
  15.4 0.7 stack.31.place_ref
  16.0 3.8 %turn_data.1 = (bf16[2,2,256,256]{3,2,1,0:T(8,128)(2,1)}, bf16[2,2,256,256]{3,2,1,0:T(8,128)(2,1)}, bf16[2,2,256,256]{3,2,1,0:T(8,128)(2,1)}, bf16[2,2,256,256]{3,2,1,0:T(8,128)(2,1)}) custom-call(s32[7]{0:T(128)} %stack.31.place_ref, bf16[2,16,128,256]{3,2,1,0:T(8,128)(2,1)} %bitcast.31), custom_call_target="tpu_custom_call" | custom-call | bytes 9000000 | tf_op jit(solution)/shard_map/turn_data/pallas_call | solution.py:274
  19.9 1.4 %collective-permute-start.8 = (bf16[2,2,256,256]{3,2,1,0:T(8,128)(2,1)}, bf16[2,2,256,256]{3,2,1,0:T(8,128)(2,1)S(1)}, u32[]{:S(2)}, u32[]{:S(2)}) collective-permute-start(bf16[2,2,256,256]{3,2,1,0:T(8,128)(2,1)} %get-tuple-element.39), channel_id=1, source_target_pairs={{0,1},{1,0},{2,3},{3,2},{4,5},{5,4},{6,7},{7,6},{8,9},{9,8},{10,11... | collective-permute-start | bytes 1572872 | tf_op jit(solution)/shard_map/ppermute | solution.py:403
  21.2 1.2 %collective-permute-start.9 = (bf16[2,2,256,256]{3,2,1,0:T(8,128)(2,1)}, bf16[2,2,256,256]{3,2,1,0:T(8,128)(2,1)}, u32[]{:S(2)}, u32[]{:S(2)}) collective-permute-start(bf16[2,2,256,256]{3,2,1,0:T(8,128)(2,1)} %get-tuple-element.40), channel_id=1, source_target_pairs={{0,2},{1,3},{2,0},{3,1},{4,6},{5,7},{6,4},{7,5},{8,10},{9,11},{10,... | collective-permute-start | bytes 1572872 | tf_op jit(solution)/shard_map/ppermute | solution.py:403
  22.4 1.7 %all-to-all-done.own0_ref = bf16[16,2,16,256]{3,2,1,0:T(8,128)(2,1)S(1)} async-done(((bf16[16,2,16,256]{3,2,1,0:T(8,128)(2,1)}), bf16[16,2,16,256]{3,2,1,0:T(8,128)(2,1)S(1)}, u32[]{:S(2)}, u32[]{:S(2)}) %all-to-all-start) | async-done | bytes 262176 | tf_op jit(solution)/shard_map/all_to_all | solution.py:400
  24.2 2.6 %collective-permute-start.1 = (bf16[16,2,16,256]{3,2,1,0:T(8,128)(2,1)S(1)}, bf16[16,2,16,256]{3,2,1,0:T(8,128)(2,1)S(1)}, u32[]{:S(2)}, u32[]{:S(2)}) collective-permute-start(bf16[16,2,16,256]{3,2,1,0:T(8,128)(2,1)S(1)} %all-to-all-done.own0_ref), channel_id=1, source_target_pairs={{0,192},{64,0},{128,64},{192,128},{1,193},{65,1},{129,65},{193,129... | collective-permute-start | bytes 786440 | tf_op jit(solution)/shard_map/ppermute | solution.py:415
  26.8 0.1 collective-permute-start.10
  26.9 3.2 %collective-permute-done.1.own1_ref = bf16[16,2,16,256]{3,2,1,0:T(8,128)(2,1)S(1)} collective-permute-done((bf16[16,2,16,256]{3,2,1,0:T(8,128)(2,1)S(1)}, bf16[16,2,16,256]{3,2,1,0:T(8,128)(2,1)S(1)}, u32[]{:S(2)}, u32[]{:S(2)}) %collective-permute-start.1) | collective-permute-done | bytes 262176 | tf_op jit(solution)/shard_map/ppermute | solution.py:415
  30.1 3.1 %collective-permute-start.3 = (bf16[16,2,16,256]{3,2,1,0:T(8,128)(2,1)S(1)}, bf16[16,2,16,256]{3,2,1,0:T(8,128)(2,1)}, u32[]{:S(2)}, u32[]{:S(2)}) collective-permute-start(bf16[16,2,16,256]{3,2,1,0:T(8,128)(2,1)S(1)} %collective-permute-done.1.own1_ref), channel_id=1, source_target_pairs={{0,192},{64,0},{128,64},{192,128},{1,193},{65,1},{129,65},{193,129... | collective-permute-start | bytes 786440 | tf_op jit(solution)/shard_map/ppermute | solution.py:416
  33.2 0.4 copy.13.col_ref
  33.7 6.4 %warp_forward.1 = bf16[16,32,256]{2,1,0:T(8,128)(2,1)} custom-call(s32[7]{0:T(128)S(1)} %copy-done.4, s32[2048,1]{1,0:T(8,128)S(1)} %copy.13.col_ref, bf16[256,64,128]{2,1,0:T(8,128)(2,1)} %bitcast.28, bf16[128,256]{1,0:T(8,128)(2,1)S(1)} %collective-permute-done.prior_ref, bf16[128,256]{1,0:T(8,128)(2,1)S(1)} %bitcast.27), custom_call_target="tpu_custom_call" | custom-call | bytes 24000000 | tf_op jit(solution)/shard_map/warp_forward/pallas_call | solution.py:274
  40.1 3.9 %all-to-all-start.1 = ((bf16[16,32,256]{2,1,0:T(8,128)(2,1)}), bf16[16,32,256]{2,1,0:T(8,128)(2,1)S(1)}, u32[]{:S(2)}, u32[]{:S(2)}) async-start(bf16[16,32,256]{2,1,0:T(8,128)(2,1)} %warp_forward.1), calls=%async_computation.1 | async-start | bytes 524288 | tf_op jit(solution)/shard_map/all_to_all | solution.py:417
  44.0 6.1 %collective-permute-start.4 = (bf16[16,2,16,256]{3,2,1,0:T(8,128)(2,1)S(1)}, bf16[16,2,16,256]{3,2,1,0:T(8,128)(2,1)}, u32[]{:S(2)}, u32[]{:S(2)}) collective-permute-start(bf16[16,2,16,256]{3,2,1,0:T(8,128)(2,1)S(1)} %all-to-all-done.own0_ref), channel_id=1, source_target_pairs={{0,16},{16,0},{1,17},{17,1},{2,18},{18,2},{3,19},{19,3},{4,20},{20... | collective-permute-start | bytes 786440 | tf_op jit(solution)/shard_map/ppermute | solution.py:419
  50.1 0.1 collective-permute-start.5
  50.2 0.4 collective-permute-start.6
  50.6 0.3 collective-permute-start.7
  50.9 0.5 collective-permute-done.4.other0_ref
  51.4 2.5 %all-to-all-done.1 = bf16[16,32,256]{2,1,0:T(8,128)(2,1)S(1)} async-done(((bf16[16,32,256]{2,1,0:T(8,128)(2,1)}), bf16[16,32,256]{2,1,0:T(8,128)(2,1)S(1)}, u32[]{:S(2)}, u32[]{:S(2)}) %all-to-all-start.1) | async-done | bytes 262176 | tf_op jit(solution)/shard_map/all_to_all | solution.py:417
  53.9 7.0 %data_gradient.1 = bf16[16,2,16,256]{3,2,1,0:T(8,128)(2,1)} custom-call(s32[7]{0:T(128)S(1)} %copy-done.4, bf16[16,2,16,256]{3,2,1,0:T(8,128)(2,1)S(1)} %bitcast.23, bf16[16,2,16,256]{3,2,1,0:T(8,128)(2,1)S(1)} %all-to-all-done.own0_ref, bf16[16,2,16,256]{3,2,1,0:T(8,128)(2,1)S(1)} %collective-permute-done.1.own1_ref, ...), custom_call_target="tpu_custom_call" | custom-call | bytes 24000000 | tf_op jit(solution)/shard_map/data_gradient/pallas_call | solution.py:274
  60.9 6.6 %all-to-all-start.2 = ((bf16[16,2,16,256]{3,2,1,0:T(8,128)(2,1)}), bf16[16,2,16,256]{3,2,1,0:T(8,128)(2,1)S(1)}, u32[]{:S(2)}, u32[]{:S(2)}) async-start(bf16[16,2,16,256]{3,2,1,0:T(8,128)(2,1)} %data_gradient.1), calls=%async_computation.2 | async-start | bytes 524288 | tf_op jit(solution)/shard_map/all_to_all | solution.py:423
  67.5 1.3 %reshape_reshape.7.row_ref = s32[1,2048]{1,0:T(1,128)S(1)} reshape(s32[256,2,4]{2,1,0:T(2,128)} %copy-done.5) | data formatting | bytes 16384 | tf_op jit(solution)/shard_map/reshape;reshape | solution.py:411
  68.8 8.4 %all-to-all-done.2 = bf16[16,2,16,256]{3,2,1,0:T(8,128)(2,1)S(1)} async-done(((bf16[16,2,16,256]{3,2,1,0:T(8,128)(2,1)}), bf16[16,2,16,256]{3,2,1,0:T(8,128)(2,1)S(1)}, u32[]{:S(2)}, u32[]{:S(2)}) %all-to-all-start.2) | async-done | bytes 262176 | tf_op jit(solution)/shard_map/all_to_all | solution.py:423
  77.3 4.8 %warp_adjoint.1 = (f32[128,256]{1,0:T(8,128)S(1)}, bf16[128,256]{1,0:T(8,128)(2,1)S(1)}) custom-call(s32[7]{0:T(128)S(1)} %copy-done.4, s32[2048,1]{1,0:T(8,128)S(1)} %copy.13.col_ref, s32[1,2048]{1,0:T(1,128)S(1)} %reshape_reshape.7.row_ref, bf16[256,64,128]{2,1,0:T(8,128)(2,1)} %bitcast.29, bf16[16,32,256]{2,1,0:T(8,128)(2,1)S(1)} %bitcast.24), custom_call_target="tpu_custom_call" | custom-call | bytes 24000000 | tf_op jit(solution)/shard_map/warp_adjoint/pallas_call | solution.py:274
  82.1 4.9 %collective-permute-start.11 = (bf16[128,256]{1,0:T(8,128)(2,1)S(1)}, bf16[128,256]{1,0:T(8,128)(2,1)S(1)}, u32[]{:S(2)}, u32[]{:S(2)}) collective-permute-start(bf16[128,256]{1,0:T(8,128)(2,1)S(1)} %get-tuple-element.56), channel_id=1, source_target_pairs={{16,0},{32,16},{48,32},{64,48},{80,64},{96,80},{112,96},{128,112},... | collective-permute-start | bytes 196616 | tf_op jit(solution)/shard_map/ppermute | solution.py:425
  86.9 3.6 %collective-permute-done.11 = bf16[128,256]{1,0:T(8,128)(2,1)S(1)} collective-permute-done((bf16[128,256]{1,0:T(8,128)(2,1)S(1)}, bf16[128,256]{1,0:T(8,128)(2,1)S(1)}, u32[]{:S(2)}, u32[]{:S(2)}) %collective-permute-start.11) | collective-permute-done | bytes 65568 | tf_op jit(solution)/shard_map/ppermute | solution.py:425
  90.5 0.7 add_bitcast_fusion
  (25 shorter events, 0.1 us)
Async XLA Ops:
  0.0 14.5 %copy-start.6 = (s32[1,256,2]{1,2,0:T(2,128)S(1)}, s32[1,256,2]{1,2,0:T(2,128)}, u32[]{:S(2)}) copy-start(s32[1,256,2]{1,2,0:T(2,128)} %param.9) | copy-start | bytes 6148
  0.0 6.1 %collective-permute-start = (bf16[128,256]{1,0:T(8,128)(2,1)}, bf16[128,256]{1,0:T(8,128)(2,1)S(1)}, u32[]{:S(2)}, u32[]{:S(2)}) collective-permute-start(bf16[128,256]{1,0:T(8,128)(2,1)} %bitcast.26), channel_id=1, source_target_pairs={{0,16},{16,32},{32,48},{48,64},{64,80},{80,96},{96,112},{112,128},... | collective-permute-start | bytes 196616 | tf_op jit(solution)/shard_map/ppermute | solution.py:397
  6.1 18.1 %all-to-all-start = ((bf16[16,2,16,256]{3,2,1,0:T(8,128)(2,1)}), bf16[16,2,16,256]{3,2,1,0:T(8,128)(2,1)S(1)}, u32[]{:S(2)}, u32[]{:S(2)}) async-start(bf16[16,2,16,256]{3,2,1,0:T(8,128)(2,1)} %pick_share.1), calls=%async_computation | async-start | bytes 524288 | tf_op jit(solution)/shard_map/all_to_all | solution.py:400
  14.4 19.2 %copy-start.3 = (bf16[1,16,8,256]{3,2,1,0:T(8,128)(2,1)S(1)}, bf16[1,16,8,256]{3,2,1,0:T(8,128)(2,1)}, u32[]{:S(2)}) copy-start(bf16[1,16,8,256]{3,2,1,0:T(8,128)(2,1)} %param.7) | copy-start | bytes 196612
  15.0 15.1 %copy-start.5 = (s32[256,2,4]{2,1,0:T(2,128)}, s32[256,2,4]{2,1,0:T(2,128)S(1)}, u32[]{:S(2)}) copy-start(s32[256,2,4]{2,1,0:T(2,128)S(1)} %broadcast_in_dim.2) | copy-start | bytes 24580
  16.0 17.6 %copy-start.4 = (s32[7]{0:T(128)S(1)}, s32[7]{0:T(128)}, u32[]{:S(2)}) copy-start(s32[7]{0:T(128)} %stack.31.place_ref) | copy-start | bytes 88
  19.9 24.1 %collective-permute-start.8 = (bf16[2,2,256,256]{3,2,1,0:T(8,128)(2,1)}, bf16[2,2,256,256]{3,2,1,0:T(8,128)(2,1)S(1)}, u32[]{:S(2)}, u32[]{:S(2)}) collective-permute-start(bf16[2,2,256,256]{3,2,1,0:T(8,128)(2,1)} %get-tuple-element.39), channel_id=1, source_target_pairs={{0,1},{1,0},{2,3},{3,2},{4,5},{5,4},{6,7},{7,6},{8,9},{9,8},{10,11... | collective-permute-start | bytes 1572872 | tf_op jit(solution)/shard_map/ppermute | solution.py:403
  21.2 28.9 %collective-permute-start.9 = (bf16[2,2,256,256]{3,2,1,0:T(8,128)(2,1)}, bf16[2,2,256,256]{3,2,1,0:T(8,128)(2,1)}, u32[]{:S(2)}, u32[]{:S(2)}) collective-permute-start(bf16[2,2,256,256]{3,2,1,0:T(8,128)(2,1)} %get-tuple-element.40), channel_id=1, source_target_pairs={{0,2},{1,3},{2,0},{3,1},{4,6},{5,7},{6,4},{7,5},{8,10},{9,11},{10,... | collective-permute-start | bytes 1572872 | tf_op jit(solution)/shard_map/ppermute | solution.py:403
  24.2 6.0 %collective-permute-start.1 = (bf16[16,2,16,256]{3,2,1,0:T(8,128)(2,1)S(1)}, bf16[16,2,16,256]{3,2,1,0:T(8,128)(2,1)S(1)}, u32[]{:S(2)}, u32[]{:S(2)}) collective-permute-start(bf16[16,2,16,256]{3,2,1,0:T(8,128)(2,1)S(1)} %all-to-all-done.own0_ref), channel_id=1, source_target_pairs={{0,192},{64,0},{128,64},{192,128},{1,193},{65,1},{129,65},{193,129... | collective-permute-start | bytes 786440 | tf_op jit(solution)/shard_map/ppermute | solution.py:415
  26.8 24.1 %collective-permute-start.10 = (bf16[2,2,256,256]{3,2,1,0:T(8,128)(2,1)}, bf16[2,2,256,256]{3,2,1,0:T(8,128)(2,1)}, u32[]{:S(2)}, u32[]{:S(2)}) collective-permute-start(bf16[2,2,256,256]{3,2,1,0:T(8,128)(2,1)} %get-tuple-element.41), channel_id=1, source_target_pairs={{0,3},{1,2},{2,1},{3,0},{4,7},{5,6},{6,5},{7,4},{8,11},{9,10},{10,... | collective-permute-start | bytes 1572872 | tf_op jit(solution)/shard_map/ppermute | solution.py:403
  26.9 23.3 %collective-permute-start.2 = (bf16[16,2,16,256]{3,2,1,0:T(8,128)(2,1)S(1)}, bf16[16,2,16,256]{3,2,1,0:T(8,128)(2,1)}, u32[]{:S(2)}, u32[]{:S(2)}) collective-permute-start(bf16[16,2,16,256]{3,2,1,0:T(8,128)(2,1)S(1)} %all-to-all-done.own0_ref), channel_id=1, source_target_pairs={{0,64},{64,128},{128,192},{192,0},{1,65},{65,129},{129,193},{193,1... | collective-permute-start | bytes 786440 | tf_op jit(solution)/shard_map/ppermute | solution.py:415
  30.1 20.5 %collective-permute-start.3 = (bf16[16,2,16,256]{3,2,1,0:T(8,128)(2,1)S(1)}, bf16[16,2,16,256]{3,2,1,0:T(8,128)(2,1)}, u32[]{:S(2)}, u32[]{:S(2)}) collective-permute-start(bf16[16,2,16,256]{3,2,1,0:T(8,128)(2,1)S(1)} %collective-permute-done.1.own1_ref), channel_id=1, source_target_pairs={{0,192},{64,0},{128,64},{192,128},{1,193},{65,1},{129,65},{193,129... | collective-permute-start | bytes 786440 | tf_op jit(solution)/shard_map/ppermute | solution.py:416
  33.6 20.3 %copy-start = (bf16[256,1024]{1,0:T(8,128)(2,1)S(1)}, bf16[256,1024]{1,0:T(8,128)(2,1)}, u32[]{:S(2)}) copy-start(bf16[256,1024]{1,0:T(8,128)(2,1)} %constant.52.clone.tables_ref) | copy-start | bytes 1572868
  33.6 20.3 %copy-start.1 = (bf16[2,2,256,256]{3,2,1,0:T(8,128)(2,1)S(1)}, bf16[2,2,256,256]{3,2,1,0:T(8,128)(2,1)}, u32[]{:S(2)}) copy-start(bf16[2,2,256,256]{3,2,1,0:T(8,128)(2,1)} %get-tuple-element.51.data0_ref) | copy-start | bytes 1572868
  33.7 20.3 %copy-start.2 = (s32[1,256,128]{2,1,0:T(8,128)S(1)}, s32[1,256,128]{2,1,0:T(8,128)}, u32[]{:S(2)}) copy-start(s32[1,256,128]{2,1,0:T(8,128)} %param.10) | copy-start | bytes 393220
  40.1 13.8 %all-to-all-start.1 = ((bf16[16,32,256]{2,1,0:T(8,128)(2,1)}), bf16[16,32,256]{2,1,0:T(8,128)(2,1)S(1)}, u32[]{:S(2)}, u32[]{:S(2)}) async-start(bf16[16,32,256]{2,1,0:T(8,128)(2,1)} %warp_forward.1), calls=%async_computation.1 | async-start | bytes 524288 | tf_op jit(solution)/shard_map/all_to_all | solution.py:417
  44.0 7.4 %collective-permute-start.4 = (bf16[16,2,16,256]{3,2,1,0:T(8,128)(2,1)S(1)}, bf16[16,2,16,256]{3,2,1,0:T(8,128)(2,1)}, u32[]{:S(2)}, u32[]{:S(2)}) collective-permute-start(bf16[16,2,16,256]{3,2,1,0:T(8,128)(2,1)S(1)} %all-to-all-done.own0_ref), channel_id=1, source_target_pairs={{0,16},{16,0},{1,17},{17,1},{2,18},{18,2},{3,19},{19,3},{4,20},{20... | collective-permute-start | bytes 786440 | tf_op jit(solution)/shard_map/ppermute | solution.py:419
  50.1 3.8 %collective-permute-start.5 = (bf16[16,2,16,256]{3,2,1,0:T(8,128)(2,1)S(1)}, bf16[16,2,16,256]{3,2,1,0:T(8,128)(2,1)}, u32[]{:S(2)}, u32[]{:S(2)}) collective-permute-start(bf16[16,2,16,256]{3,2,1,0:T(8,128)(2,1)S(1)} %collective-permute-done.1.own1_ref), channel_id=1, source_target_pairs={{0,16},{16,0},{1,17},{17,1},{2,18},{18,2},{3,19},{19,3},{4,20},{20... | collective-permute-start | bytes 786440 | tf_op jit(solution)/shard_map/ppermute | solution.py:419
  50.2 3.6 %collective-permute-start.6 = (bf16[16,2,16,256]{3,2,1,0:T(8,128)(2,1)}, bf16[16,2,16,256]{3,2,1,0:T(8,128)(2,1)}, u32[]{:S(2)}, u32[]{:S(2)}) collective-permute-start(bf16[16,2,16,256]{3,2,1,0:T(8,128)(2,1)} %collective-permute-done.2.own2_ref), channel_id=1, source_target_pairs={{0,16},{16,0},{1,17},{17,1},{2,18},{18,2},{3,19},{19,3},{4,20},{20... | collective-permute-start | bytes 786440 | tf_op jit(solution)/shard_map/ppermute | solution.py:419
  50.6 3.2 %collective-permute-start.7 = (bf16[16,2,16,256]{3,2,1,0:T(8,128)(2,1)}, bf16[16,2,16,256]{3,2,1,0:T(8,128)(2,1)}, u32[]{:S(2)}, u32[]{:S(2)}) collective-permute-start(bf16[16,2,16,256]{3,2,1,0:T(8,128)(2,1)} %collective-permute-done.3.own3_ref), channel_id=1, source_target_pairs={{0,16},{16,0},{1,17},{17,1},{2,18},{18,2},{3,19},{19,3},{4,20},{20... | collective-permute-start | bytes 786440 | tf_op jit(solution)/shard_map/ppermute | solution.py:419
  60.9 16.3 %all-to-all-start.2 = ((bf16[16,2,16,256]{3,2,1,0:T(8,128)(2,1)}), bf16[16,2,16,256]{3,2,1,0:T(8,128)(2,1)S(1)}, u32[]{:S(2)}, u32[]{:S(2)}) async-start(bf16[16,2,16,256]{3,2,1,0:T(8,128)(2,1)} %data_gradient.1), calls=%async_computation.2 | async-start | bytes 524288 | tf_op jit(solution)/shard_map/all_to_all | solution.py:423
  82.1 8.4 %collective-permute-start.11 = (bf16[128,256]{1,0:T(8,128)(2,1)S(1)}, bf16[128,256]{1,0:T(8,128)(2,1)S(1)}, u32[]{:S(2)}, u32[]{:S(2)}) collective-permute-start(bf16[128,256]{1,0:T(8,128)(2,1)S(1)} %get-tuple-element.56), channel_id=1, source_target_pairs={{16,0},{32,16},{48,32},{64,48},{80,64},{96,80},{112,96},{128,112},... | collective-permute-start | bytes 196616 | tf_op jit(solution)/shard_map/ppermute | solution.py:425

commit v5 on v4

--- a/solution.py
+++ b/solution.py
@@ -396,7 +396,8 @@
     current = cine_image.reshape(128, 256)
     prior = lax.ppermute(current, loop_axes, forward)
 
-    sens, prior, kspace_data = lax.optimization_barrier((pick_share((row * 2 + core).reshape(1), sensitivity), prior, kspace_data))
+    sens = pick_share((row * 2 + core).reshape(1), sensitivity)
+    prior, kspace_data = lax.optimization_barrier((prior, kspace_data))
     sens = lax.all_to_all(sens, coil, 0, 0, tiled=True)
     measured = turn_data(place, kspace_data)
     measured = [

time: 91.7 us -> 95 us (1.036)
  starting transfers between devices: 43.2 us -> 48.7 us
  waiting for transfers between devices: 19.9 us -> 17.8 us
    all_to_all x1, starting transfers between devices: 3.94 us -> 7.14 us  [on_device(): lax.all_to_all(moved, coil, 0, 0, tiled=True).reshape(16, 2, 16, 256)]
    all_to_all x1, waiting for transfers between devices: 1.75 us -> 0.01 us  [on_device(): sens = lax.all_to_all(sens, coil, 0, 0, tiled=True)]
    all_to_all x1, starting transfers between devices: 8.32 us -> 10 us  [on_device(): sens = lax.all_to_all(sens, coil, 0, 0, tiled=True)]
  transfers between devices with their start and end apart: 15 -> 15, of which waited for: 6 -> 5; matrix products, arithmetic and copies ran while one was open for 3% -> 3% of each run, Pallas kernels for 13% -> 11%
where the time goes in v5:
time: 95 us; the launch traced here: 94.5 us
  starting transfers between devices  48.7 us (51%)
  Pallas kernels  24 us (25%)
  waiting for transfers between devices  17.8 us (19%)
  local copies, waits for them, and re-layouts  3.18 us (3%)
    pallas_call x5, Pallas kernels, call(): pl.pallas_call(kernel, grid_spec=pltpu.PrefetchScalarGridSpec(num_scalar_...  24 us
    all_to_all x1, starting transfers between devices, on_device(): sens = lax.all_to_all(sens, coil, 0, 0, tiled=True)  10 us
    all_to_all x1, waiting for transfers between devices, on_device(): parts = lax.all_to_all(parts, coil, 0, 0, tiled=True).reshape(16, 32, 256)  8.42 us
    all_to_all x1, starting transfers between devices, on_device(): parts = lax.all_to_all(parts, coil, 0, 0, tiled=True).reshape(16, 32, 256)  7.35 us
    ppermute x4, starting transfers between devices, on_device(): other = [lax.ppermute(piece, 'core', [(0, 1), (1, 0)]) for piece in sens]  7.32 us
    all_to_all x1, starting transfers between devices, on_device(): lax.all_to_all(moved, coil, 0, 0, tiled=True).reshape(16, 2, 16, 256)  7.14 us
    ppermute x1, starting transfers between devices, on_device(): from_next = lax.ppermute(pulled, loop_axes, backward)  4.82 us
    ppermute x1, waiting for transfers between devices, on_device(): from_next = lax.ppermute(pulled, loop_axes, backward)  4.32 us
  transfers between devices with their start and end apart: 15, of which 5 were waited for; matrix products, arithmetic and copies ran while one was open for 3% of the time, Pallas kernels for 11%

profile of v5, /device:TPU:1, one launch (start us, length us, event | category | flops | bytes accessed | tf_op | source)
XLA Modules:
  0.0 94.5 jit_solution(15766993046192000225)
XLA Ops:
  0.0 2.0 %pick_share.1 = bf16[16,2,16,256]{3,2,1,0:T(8,128)(2,1)} custom-call(s32[1]{0:T(128)} %bitcast.8.place_ref, bf16[4,4,2,128,256]{4,3,2,1,0:T(8,128)(2,1)} %bitcast.30), custom_call_target="tpu_custom_call" | custom-call | bytes 3000000 | tf_op jit(solution)/shard_map/pick_share/pallas_call | solution.py:274
  2.0 10.0 %all-to-all-start = ((bf16[16,2,16,256]{3,2,1,0:T(8,128)(2,1)}), bf16[16,2,16,256]{3,2,1,0:T(8,128)(2,1)S(1)}, u32[]{:S(2)}, u32[]{:S(2)}) async-start(bf16[16,2,16,256]{3,2,1,0:T(8,128)(2,1)} %pick_share.1), calls=%async_computation | async-start | bytes 524288 | tf_op jit(solution)/shard_map/all_to_all | solution.py:401
  12.1 3.4 %collective-permute-start = (bf16[128,256]{1,0:T(8,128)(2,1)S(1)}, bf16[128,256]{1,0:T(8,128)(2,1)S(1)}, u32[]{:S(2)}, u32[]{:S(2)}) collective-permute-start(bf16[128,256]{1,0:T(8,128)(2,1)S(1)} %bitcast.26), channel_id=1, source_target_pairs={{0,16},{16,32},{32,48},{48,64},{64,80},{80,96},{96,112},{112,128},... | collective-permute-start | bytes 196616 | tf_op jit(solution)/shard_map/ppermute | solution.py:397
  15.4 0.1 copy.10
  15.6 0.3 broadcast_in_dim.2
  15.9 0.3 reshape_reshape.6
  16.3 0.7 stack.31.place_ref
  17.0 3.8 %turn_data.1 = (bf16[2,2,256,256]{3,2,1,0:T(8,128)(2,1)}, bf16[2,2,256,256]{3,2,1,0:T(8,128)(2,1)}, bf16[2,2,256,256]{3,2,1,0:T(8,128)(2,1)}, bf16[2,2,256,256]{3,2,1,0:T(8,128)(2,1)}) custom-call(s32[7]{0:T(128)} %stack.31.place_ref, bf16[2,16,128,256]{3,2,1,0:T(8,128)(2,1)} %bitcast.31), custom_call_target="tpu_custom_call" | custom-call | bytes 9000000 | tf_op jit(solution)/shard_map/turn_data/pallas_call | solution.py:274
  20.7 1.0 %collective-permute-start.8 = (bf16[2,2,256,256]{3,2,1,0:T(8,128)(2,1)}, bf16[2,2,256,256]{3,2,1,0:T(8,128)(2,1)S(1)}, u32[]{:S(2)}, u32[]{:S(2)}) collective-permute-start(bf16[2,2,256,256]{3,2,1,0:T(8,128)(2,1)} %get-tuple-element.37), channel_id=1, source_target_pairs={{0,1},{1,0},{2,3},{3,2},{4,5},{5,4},{6,7},{7,6},{8,9},{9,8},{10,11... | collective-permute-start | bytes 1572872 | tf_op jit(solution)/shard_map/ppermute | solution.py:404
  21.8 1.2 %collective-permute-start.9 = (bf16[2,2,256,256]{3,2,1,0:T(8,128)(2,1)}, bf16[2,2,256,256]{3,2,1,0:T(8,128)(2,1)}, u32[]{:S(2)}, u32[]{:S(2)}) collective-permute-start(bf16[2,2,256,256]{3,2,1,0:T(8,128)(2,1)} %get-tuple-element.38), channel_id=1, source_target_pairs={{0,2},{1,3},{2,0},{3,1},{4,6},{5,7},{6,4},{7,5},{8,10},{9,11},{10,... | collective-permute-start | bytes 1572872 | tf_op jit(solution)/shard_map/ppermute | solution.py:404
  22.9 2.8 %collective-permute-start.1 = (bf16[16,2,16,256]{3,2,1,0:T(8,128)(2,1)S(1)}, bf16[16,2,16,256]{3,2,1,0:T(8,128)(2,1)S(1)}, u32[]{:S(2)}, u32[]{:S(2)}) collective-permute-start(bf16[16,2,16,256]{3,2,1,0:T(8,128)(2,1)S(1)} %all-to-all-done.own0_ref), channel_id=1, source_target_pairs={{0,192},{64,0},{128,64},{192,128},{1,193},{65,1},{129,65},{193,129... | collective-permute-start | bytes 786440 | tf_op jit(solution)/shard_map/ppermute | solution.py:416
  25.7 0.6 collective-permute-start.10
  26.3 2.7 %collective-permute-done.1.own1_ref = bf16[16,2,16,256]{3,2,1,0:T(8,128)(2,1)S(1)} collective-permute-done((bf16[16,2,16,256]{3,2,1,0:T(8,128)(2,1)S(1)}, bf16[16,2,16,256]{3,2,1,0:T(8,128)(2,1)S(1)}, u32[]{:S(2)}, u32[]{:S(2)}) %collective-permute-start.1) | collective-permute-done | bytes 262176 | tf_op jit(solution)/shard_map/ppermute | solution.py:416
  29.0 3.1 %collective-permute-start.3 = (bf16[16,2,16,256]{3,2,1,0:T(8,128)(2,1)S(1)}, bf16[16,2,16,256]{3,2,1,0:T(8,128)(2,1)}, u32[]{:S(2)}, u32[]{:S(2)}) collective-permute-start(bf16[16,2,16,256]{3,2,1,0:T(8,128)(2,1)S(1)} %collective-permute-done.1.own1_ref), channel_id=1, source_target_pairs={{0,192},{64,0},{128,64},{192,128},{1,193},{65,1},{129,65},{193,129... | collective-permute-start | bytes 786440 | tf_op jit(solution)/shard_map/ppermute | solution.py:417
  32.1 0.4 copy.13.col_ref
  32.5 0.0 copy-start
  32.5 6.4 %warp_forward.1 = bf16[16,32,256]{2,1,0:T(8,128)(2,1)} custom-call(s32[7]{0:T(128)S(1)} %copy-done.4, s32[2048,1]{1,0:T(8,128)S(1)} %copy.13.col_ref, bf16[256,64,128]{2,1,0:T(8,128)(2,1)} %bitcast.28, bf16[128,256]{1,0:T(8,128)(2,1)S(1)} %collective-permute-done.prior_ref, bf16[128,256]{1,0:T(8,128)(2,1)S(1)} %bitcast.27), custom_call_target="tpu_custom_call" | custom-call | bytes 24000000 | tf_op jit(solution)/shard_map/warp_forward/pallas_call | solution.py:274
  38.9 7.1 %all-to-all-start.1 = ((bf16[16,32,256]{2,1,0:T(8,128)(2,1)}), bf16[16,32,256]{2,1,0:T(8,128)(2,1)S(1)}, u32[]{:S(2)}, u32[]{:S(2)}) async-start(bf16[16,32,256]{2,1,0:T(8,128)(2,1)} %warp_forward.1), calls=%async_computation.1 | async-start | bytes 524288 | tf_op jit(solution)/shard_map/all_to_all | solution.py:418
  46.1 6.5 %collective-permute-start.4 = (bf16[16,2,16,256]{3,2,1,0:T(8,128)(2,1)S(1)}, bf16[16,2,16,256]{3,2,1,0:T(8,128)(2,1)}, u32[]{:S(2)}, u32[]{:S(2)}) collective-permute-start(bf16[16,2,16,256]{3,2,1,0:T(8,128)(2,1)S(1)} %all-to-all-done.own0_ref), channel_id=1, source_target_pairs={{0,16},{16,0},{1,17},{17,1},{2,18},{18,2},{3,19},{19,3},{4,20},{20... | collective-permute-start | bytes 786440 | tf_op jit(solution)/shard_map/ppermute | solution.py:420
  52.6 0.1 collective-permute-start.5
  52.8 0.4 collective-permute-start.6
  53.2 0.3 collective-permute-start.7
  53.4 0.5 collective-permute-done.4.other0_ref
  53.9 1.8 %all-to-all-done.1 = bf16[16,32,256]{2,1,0:T(8,128)(2,1)S(1)} async-done(((bf16[16,32,256]{2,1,0:T(8,128)(2,1)}), bf16[16,32,256]{2,1,0:T(8,128)(2,1)S(1)}, u32[]{:S(2)}, u32[]{:S(2)}) %all-to-all-start.1) | async-done | bytes 262176 | tf_op jit(solution)/shard_map/all_to_all | solution.py:418
  55.8 7.0 %data_gradient.1 = bf16[16,2,16,256]{3,2,1,0:T(8,128)(2,1)} custom-call(s32[7]{0:T(128)S(1)} %copy-done.4, bf16[16,2,16,256]{3,2,1,0:T(8,128)(2,1)S(1)} %bitcast.23, bf16[16,2,16,256]{3,2,1,0:T(8,128)(2,1)S(1)} %all-to-all-done.own0_ref, bf16[16,2,16,256]{3,2,1,0:T(8,128)(2,1)S(1)} %collective-permute-done.1.own1_ref, ...), custom_call_target="tpu_custom_call" | custom-call | bytes 24000000 | tf_op jit(solution)/shard_map/data_gradient/pallas_call | solution.py:274
  62.8 7.4 %all-to-all-start.2 = ((bf16[16,2,16,256]{3,2,1,0:T(8,128)(2,1)}), bf16[16,2,16,256]{3,2,1,0:T(8,128)(2,1)S(1)}, u32[]{:S(2)}, u32[]{:S(2)}) async-start(bf16[16,2,16,256]{3,2,1,0:T(8,128)(2,1)} %data_gradient.1), calls=%async_computation.2 | async-start | bytes 524288 | tf_op jit(solution)/shard_map/all_to_all | solution.py:424
  70.1 1.3 %reshape_reshape.7.row_ref = s32[1,2048]{1,0:T(1,128)S(1)} reshape(s32[256,2,4]{2,1,0:T(2,128)} %copy-done.5) | data formatting | bytes 16384 | tf_op jit(solution)/shard_map/reshape;reshape | solution.py:412
  71.4 8.4 %all-to-all-done.2 = bf16[16,2,16,256]{3,2,1,0:T(8,128)(2,1)S(1)} async-done(((bf16[16,2,16,256]{3,2,1,0:T(8,128)(2,1)}), bf16[16,2,16,256]{3,2,1,0:T(8,128)(2,1)S(1)}, u32[]{:S(2)}, u32[]{:S(2)}) %all-to-all-start.2) | async-done | bytes 262176 | tf_op jit(solution)/shard_map/all_to_all | solution.py:424
  79.8 4.8 %warp_adjoint.1 = (f32[128,256]{1,0:T(8,128)S(1)}, bf16[128,256]{1,0:T(8,128)(2,1)S(1)}) custom-call(s32[7]{0:T(128)S(1)} %copy-done.4, s32[2048,1]{1,0:T(8,128)S(1)} %copy.13.col_ref, s32[1,2048]{1,0:T(1,128)S(1)} %reshape_reshape.7.row_ref, bf16[256,64,128]{2,1,0:T(8,128)(2,1)} %bitcast.29, bf16[16,32,256]{2,1,0:T(8,128)(2,1)S(1)} %bitcast.24), custom_call_target="tpu_custom_call" | custom-call | bytes 24000000 | tf_op jit(solution)/shard_map/warp_adjoint/pallas_call | solution.py:274
  84.7 4.8 %collective-permute-start.11 = (bf16[128,256]{1,0:T(8,128)(2,1)S(1)}, bf16[128,256]{1,0:T(8,128)(2,1)S(1)}, u32[]{:S(2)}, u32[]{:S(2)}) collective-permute-start(bf16[128,256]{1,0:T(8,128)(2,1)S(1)} %get-tuple-element.54), channel_id=1, source_target_pairs={{16,0},{32,16},{48,32},{64,48},{80,64},{96,80},{112,96},{128,112},... | collective-permute-start | bytes 196616 | tf_op jit(solution)/shard_map/ppermute | solution.py:426
  89.5 4.3 %collective-permute-done.11 = bf16[128,256]{1,0:T(8,128)(2,1)S(1)} collective-permute-done((bf16[128,256]{1,0:T(8,128)(2,1)S(1)}, bf16[128,256]{1,0:T(8,128)(2,1)S(1)}, u32[]{:S(2)}, u32[]{:S(2)}) %collective-permute-start.11) | collective-permute-done | bytes 65568 | tf_op jit(solution)/shard_map/ppermute | solution.py:426
  93.8 0.7 add_bitcast_fusion
  (25 shorter events, 0.1 us)
Async XLA Ops:
  0.0 12.1 %copy-start.3 = (bf16[1,16,8,256]{3,2,1,0:T(8,128)(2,1)S(1)}, bf16[1,16,8,256]{3,2,1,0:T(8,128)(2,1)}, u32[]{:S(2)}) copy-start(bf16[1,16,8,256]{3,2,1,0:T(8,128)(2,1)} %param.7) | copy-start | bytes 196612
  0.0 15.4 %copy-start.6 = (s32[1,256,2]{1,2,0:T(2,128)S(1)}, s32[1,256,2]{1,2,0:T(2,128)}, u32[]{:S(2)}) copy-start(s32[1,256,2]{1,2,0:T(2,128)} %param.9) | copy-start | bytes 6148
  2.0 20.9 %all-to-all-start = ((bf16[16,2,16,256]{3,2,1,0:T(8,128)(2,1)}), bf16[16,2,16,256]{3,2,1,0:T(8,128)(2,1)S(1)}, u32[]{:S(2)}, u32[]{:S(2)}) async-start(bf16[16,2,16,256]{3,2,1,0:T(8,128)(2,1)} %pick_share.1), calls=%async_computation | async-start | bytes 524288 | tf_op jit(solution)/shard_map/all_to_all | solution.py:401
  12.1 4.9 %collective-permute-start = (bf16[128,256]{1,0:T(8,128)(2,1)S(1)}, bf16[128,256]{1,0:T(8,128)(2,1)S(1)}, u32[]{:S(2)}, u32[]{:S(2)}) collective-permute-start(bf16[128,256]{1,0:T(8,128)(2,1)S(1)} %bitcast.26), channel_id=1, source_target_pairs={{0,16},{16,32},{32,48},{48,64},{64,80},{80,96},{96,112},{112,128},... | collective-permute-start | bytes 196616 | tf_op jit(solution)/shard_map/ppermute | solution.py:397
  15.9 13.1 %copy-start.5 = (s32[256,2,4]{2,1,0:T(2,128)}, s32[256,2,4]{2,1,0:T(2,128)S(1)}, u32[]{:S(2)}) copy-start(s32[256,2,4]{2,1,0:T(2,128)S(1)} %broadcast_in_dim.2) | copy-start | bytes 24580
  17.0 15.6 %copy-start.4 = (s32[7]{0:T(128)S(1)}, s32[7]{0:T(128)}, u32[]{:S(2)}) copy-start(s32[7]{0:T(128)} %stack.31.place_ref) | copy-start | bytes 88
  20.7 25.4 %collective-permute-start.8 = (bf16[2,2,256,256]{3,2,1,0:T(8,128)(2,1)}, bf16[2,2,256,256]{3,2,1,0:T(8,128)(2,1)S(1)}, u32[]{:S(2)}, u32[]{:S(2)}) collective-permute-start(bf16[2,2,256,256]{3,2,1,0:T(8,128)(2,1)} %get-tuple-element.37), channel_id=1, source_target_pairs={{0,1},{1,0},{2,3},{3,2},{4,5},{5,4},{6,7},{7,6},{8,9},{9,8},{10,11... | collective-permute-start | bytes 1572872 | tf_op jit(solution)/shard_map/ppermute | solution.py:404
  21.8 30.9 %collective-permute-start.9 = (bf16[2,2,256,256]{3,2,1,0:T(8,128)(2,1)}, bf16[2,2,256,256]{3,2,1,0:T(8,128)(2,1)}, u32[]{:S(2)}, u32[]{:S(2)}) collective-permute-start(bf16[2,2,256,256]{3,2,1,0:T(8,128)(2,1)} %get-tuple-element.38), channel_id=1, source_target_pairs={{0,2},{1,3},{2,0},{3,1},{4,6},{5,7},{6,4},{7,5},{8,10},{9,11},{10,... | collective-permute-start | bytes 1572872 | tf_op jit(solution)/shard_map/ppermute | solution.py:404
  22.9 6.1 %collective-permute-start.1 = (bf16[16,2,16,256]{3,2,1,0:T(8,128)(2,1)S(1)}, bf16[16,2,16,256]{3,2,1,0:T(8,128)(2,1)S(1)}, u32[]{:S(2)}, u32[]{:S(2)}) collective-permute-start(bf16[16,2,16,256]{3,2,1,0:T(8,128)(2,1)S(1)} %all-to-all-done.own0_ref), channel_id=1, source_target_pairs={{0,192},{64,0},{128,64},{192,128},{1,193},{65,1},{129,65},{193,129... | collective-permute-start | bytes 786440 | tf_op jit(solution)/shard_map/ppermute | solution.py:416
  25.7 27.7 %collective-permute-start.10 = (bf16[2,2,256,256]{3,2,1,0:T(8,128)(2,1)}, bf16[2,2,256,256]{3,2,1,0:T(8,128)(2,1)}, u32[]{:S(2)}, u32[]{:S(2)}) collective-permute-start(bf16[2,2,256,256]{3,2,1,0:T(8,128)(2,1)} %get-tuple-element.39), channel_id=1, source_target_pairs={{0,3},{1,2},{2,1},{3,0},{4,7},{5,6},{6,5},{7,4},{8,11},{9,10},{10,... | collective-permute-start | bytes 1572872 | tf_op jit(solution)/shard_map/ppermute | solution.py:404
  26.3 26.5 %collective-permute-start.2 = (bf16[16,2,16,256]{3,2,1,0:T(8,128)(2,1)S(1)}, bf16[16,2,16,256]{3,2,1,0:T(8,128)(2,1)}, u32[]{:S(2)}, u32[]{:S(2)}) collective-permute-start(bf16[16,2,16,256]{3,2,1,0:T(8,128)(2,1)S(1)} %all-to-all-done.own0_ref), channel_id=1, source_target_pairs={{0,64},{64,128},{128,192},{192,0},{1,65},{65,129},{129,193},{193,1... | collective-permute-start | bytes 786440 | tf_op jit(solution)/shard_map/ppermute | solution.py:416
  29.0 24.1 %collective-permute-start.3 = (bf16[16,2,16,256]{3,2,1,0:T(8,128)(2,1)S(1)}, bf16[16,2,16,256]{3,2,1,0:T(8,128)(2,1)}, u32[]{:S(2)}, u32[]{:S(2)}) collective-permute-start(bf16[16,2,16,256]{3,2,1,0:T(8,128)(2,1)S(1)} %collective-permute-done.1.own1_ref), channel_id=1, source_target_pairs={{0,192},{64,0},{128,64},{192,128},{1,193},{65,1},{129,65},{193,129... | collective-permute-start | bytes 786440 | tf_op jit(solution)/shard_map/ppermute | solution.py:417
  32.5 23.2 %copy-start = (bf16[256,1024]{1,0:T(8,128)(2,1)S(1)}, bf16[256,1024]{1,0:T(8,128)(2,1)}, u32[]{:S(2)}) copy-start(bf16[256,1024]{1,0:T(8,128)(2,1)} %constant.52.clone.tables_ref) | copy-start | bytes 1572868
  32.5 23.2 %copy-start.1 = (bf16[2,2,256,256]{3,2,1,0:T(8,128)(2,1)S(1)}, bf16[2,2,256,256]{3,2,1,0:T(8,128)(2,1)}, u32[]{:S(2)}) copy-start(bf16[2,2,256,256]{3,2,1,0:T(8,128)(2,1)} %get-tuple-element.49.data0_ref) | copy-start | bytes 1572868
  32.5 23.2 %copy-start.2 = (s32[1,256,128]{2,1,0:T(8,128)S(1)}, s32[1,256,128]{2,1,0:T(8,128)}, u32[]{:S(2)}) copy-start(s32[1,256,128]{2,1,0:T(8,128)} %param.10) | copy-start | bytes 393220
  38.9 16.8 %all-to-all-start.1 = ((bf16[16,32,256]{2,1,0:T(8,128)(2,1)}), bf16[16,32,256]{2,1,0:T(8,128)(2,1)S(1)}, u32[]{:S(2)}, u32[]{:S(2)}) async-start(bf16[16,32,256]{2,1,0:T(8,128)(2,1)} %warp_forward.1), calls=%async_computation.1 | async-start | bytes 524288 | tf_op jit(solution)/shard_map/all_to_all | solution.py:418
  46.1 7.8 %collective-permute-start.4 = (bf16[16,2,16,256]{3,2,1,0:T(8,128)(2,1)S(1)}, bf16[16,2,16,256]{3,2,1,0:T(8,128)(2,1)}, u32[]{:S(2)}, u32[]{:S(2)}) collective-permute-start(bf16[16,2,16,256]{3,2,1,0:T(8,128)(2,1)S(1)} %all-to-all-done.own0_ref), channel_id=1, source_target_pairs={{0,16},{16,0},{1,17},{17,1},{2,18},{18,2},{3,19},{19,3},{4,20},{20... | collective-permute-start | bytes 786440 | tf_op jit(solution)/shard_map/ppermute | solution.py:420
  52.6 3.1 %collective-permute-start.5 = (bf16[16,2,16,256]{3,2,1,0:T(8,128)(2,1)S(1)}, bf16[16,2,16,256]{3,2,1,0:T(8,128)(2,1)}, u32[]{:S(2)}, u32[]{:S(2)}) collective-permute-start(bf16[16,2,16,256]{3,2,1,0:T(8,128)(2,1)S(1)} %collective-permute-done.1.own1_ref), channel_id=1, source_target_pairs={{0,16},{16,0},{1,17},{17,1},{2,18},{18,2},{3,19},{19,3},{4,20},{20... | collective-permute-start | bytes 786440 | tf_op jit(solution)/shard_map/ppermute | solution.py:420
  52.8 3.0 %collective-permute-start.6 = (bf16[16,2,16,256]{3,2,1,0:T(8,128)(2,1)}, bf16[16,2,16,256]{3,2,1,0:T(8,128)(2,1)}, u32[]{:S(2)}, u32[]{:S(2)}) collective-permute-start(bf16[16,2,16,256]{3,2,1,0:T(8,128)(2,1)} %collective-permute-done.2.own2_ref), channel_id=1, source_target_pairs={{0,16},{16,0},{1,17},{17,1},{2,18},{18,2},{3,19},{19,3},{4,20},{20... | collective-permute-start | bytes 786440 | tf_op jit(solution)/shard_map/ppermute | solution.py:420
  53.2 2.6 %collective-permute-start.7 = (bf16[16,2,16,256]{3,2,1,0:T(8,128)(2,1)}, bf16[16,2,16,256]{3,2,1,0:T(8,128)(2,1)}, u32[]{:S(2)}, u32[]{:S(2)}) collective-permute-start(bf16[16,2,16,256]{3,2,1,0:T(8,128)(2,1)} %collective-permute-done.3.own3_ref), channel_id=1, source_target_pairs={{0,16},{16,0},{1,17},{17,1},{2,18},{18,2},{3,19},{19,3},{4,20},{20... | collective-permute-start | bytes 786440 | tf_op jit(solution)/shard_map/ppermute | solution.py:420
  62.8 17.1 %all-to-all-start.2 = ((bf16[16,2,16,256]{3,2,1,0:T(8,128)(2,1)}), bf16[16,2,16,256]{3,2,1,0:T(8,128)(2,1)S(1)}, u32[]{:S(2)}, u32[]{:S(2)}) async-start(bf16[16,2,16,256]{3,2,1,0:T(8,128)(2,1)} %data_gradient.1), calls=%async_computation.2 | async-start | bytes 524288 | tf_op jit(solution)/shard_map/all_to_all | solution.py:424
  84.7 9.1 %collective-permute-start.11 = (bf16[128,256]{1,0:T(8,128)(2,1)S(1)}, bf16[128,256]{1,0:T(8,128)(2,1)S(1)}, u32[]{:S(2)}, u32[]{:S(2)}) collective-permute-start(bf16[128,256]{1,0:T(8,128)(2,1)S(1)} %get-tuple-element.54), channel_id=1, source_target_pairs={{16,0},{32,16},{48,32},{64,48},{80,64},{96,80},{112,96},{128,112},... | collective-permute-start | bytes 196616 | tf_op jit(solution)/shard_map/ppermute | solution.py:426
